TPU v7x, 32 devices: a whole 2x2x4 slice. The times are simulated.
32 devices in a mesh: row: 4 (over z), col: 8 (over y, x, core).
Axes of the slice: x: 2, y: 2, z: 4, core: 2. Of those that a mesh axis runs over, the one named last changes fastest.
Arguments:
- hidden_in: bfloat16 [1024, 1792], P('col', 'row'), may hold values from -6 to 6
- attn_gain: float32 [1792], replicated, may hold values from 0.1 to 1.9
- mlp_gain: float32 [1792], replicated, may hold values from 0.1 to 1.9
- w_query: bfloat16 [1792, 256], P(None, 'row'), may hold values from -0.125 to 0.125
- w_key: bfloat16 [1792, 256], P(None, 'row'), may hold values from -0.125 to 0.125
- w_value: bfloat16 [1792, 1792], P(None, 'row'), may hold values from -0.125 to 0.125
- w_out: bfloat16 [1792, 1792], P('row'), may hold values from -0.1875 to 0.1875
- w_gate: bfloat16 [1792, 3584], P(None, 'row'), may hold values from -0.125 to 0.125
- w_up: bfloat16 [1792, 3584], P(None, 'row'), may hold values from -0.125 to 0.125
- w_down: bfloat16 [3584, 1792], P('row'), may hold values from -0.125 to 0.125
- page_states: bfloat16 [128, 16, 273, 112], P('col', 'row'), may hold values from -16 to 16
- page_norms: float32 [128, 16, 273], P('col', 'row'), as said below
- page_home: int32 [128, 1], P('col'), may hold values from 0 to 7; in each aligned block of 16 rows (0 to 15, 16 to 31, ...) at most 4 rows name the same one
- page_request: int32 [128], P('col'), may hold values from 0 to 1
- parents: int32 [16, 64], P('col'), may hold values from 0 to 62, as said below
- accepted: int32 [16], P('col'), may hold values from 0 to 63
Outputs:
- hidden_out: bfloat16 [1024, 1792], P('col', 'row')
- new_states: bfloat16 [16, 16, 273, 112], P('col', 'row')
- new_norms: float32 [16, 16, 273], P('col', 'row')
Inputs may be any that keep to these rules, and one draw needn't show every extreme that they name: Among the 16 slots of one device at most 4 have the same page_home, and in every draw some device has exactly 4. parents[r, 0] = 0, parents[r, i] < i for i >= 1, and the last node's parent is the node before it. Each page_norms[s, h] is a factor of 2 to 16 times the mean of phi over eight vectors, so phi(u) . page_norms[s, h] >= 1 for every vector u.
All inputs are finite; a program needn't handle non-finite values.
Results may differ from a plain program's by a relative error of at most 0.023.
Values may be sent and summed in bfloat16 or wider, within the bound.
A program may use at most 128 MiB of HBM per device.

v0:
```python
import math

import jax
import jax.numpy as jnp
from jax import lax
from jax.sharding import PartitionSpec as P

epsilon = 1e-05


def feature_map(vectors):
    width_in = vectors.shape[-1]
    linear = vectors * width_in ** (-0.25)
    square = vectors[..., :, None] * vectors[..., None, :] * (2.0 * width_in) ** (-0.5)
    square = square.reshape(vectors.shape[:-1] + (width_in * width_in,))
    leading = jnp.ones(vectors.shape[:-1] + (1,), vectors.dtype)
    return jnp.concatenate([leading, linear, square], axis=-1)


def rms_norm(hidden, gain):
    mean_square = jnp.mean(hidden * hidden, axis=-1, keepdims=True)
    return hidden * lax.rsqrt(mean_square + epsilon) * gain


def ancestors(parents):
    nodes = parents.shape[-1]
    node_ids = jnp.arange(nodes, dtype=jnp.int32)
    linked = (parents[..., :, None] == node_ids[None, :]) | (node_ids[:, None] == node_ids[None, :])
    reached = linked.astype(jnp.float32)
    for repeat in range(max(1, (nodes - 1).bit_length())):
        reached = jnp.minimum(
            jnp.einsum("rij,rjk->rik", reached, reached, precision=lax.Precision.HIGHEST), 1.0
        )
    return reached


def pack_slots(homes, requests, col_count, capacity):
    slot_count = homes.shape[0]
    slot_ids = jnp.arange(slot_count, dtype=jnp.int32)
    same_home = (homes[:, None] == homes[None, :]) & (slot_ids[None, :] < slot_ids[:, None])
    ranks = jnp.sum(same_home.astype(jnp.int32), axis=1)
    places = homes * capacity + ranks
    targets = jnp.arange(col_count * capacity, dtype=jnp.int32)
    packer = (targets[:, None] == places[None, :]).astype(jnp.float32)
    labels = (
        jnp.dot(packer, (requests + 1).astype(jnp.float32), precision=lax.Precision.HIGHEST) - 1.0
    )
    return (packer, labels)


def local(
    hidden_in,
    attn_gain,
    mlp_gain,
    w_query,
    w_key,
    w_value,
    w_out,
    w_gate,
    w_up,
    w_down,
    page_states,
    page_norms,
    page_home,
    page_request,
    parents,
    accepted,
):
    highest = lax.Precision.HIGHEST
    local_heads = page_states.shape[1]
    feat_width = w_query.shape[1] // local_heads
    value_width = w_value.shape[1] // local_heads
    req_local = parents.shape[0]
    nodes = parents.shape[1]
    tok_local = hidden_in.shape[0]
    slot_count = page_states.shape[0]
    col_count = lax.axis_size("col")
    row_count = lax.axis_size("row")
    capacity = max(2, 2 * slot_count // col_count)
    row_index = lax.axis_index("row")
    gathered = lax.all_gather(hidden_in, "row", axis=1, tiled=True)
    hidden = gathered.astype(jnp.float32)
    normed = rms_norm(hidden, attn_gain).astype(jnp.bfloat16)
    queries = jnp.dot(normed, w_query, preferred_element_type=jnp.float32).astype(jnp.bfloat16)
    key_rows = jnp.dot(normed, w_key, preferred_element_type=jnp.float32).astype(jnp.bfloat16)
    values = jnp.dot(normed, w_value, preferred_element_type=jnp.float32).astype(jnp.bfloat16)
    query_heads = queries.reshape(req_local, nodes, local_heads, feat_width)
    key_heads = key_rows.reshape(req_local, nodes, local_heads, feat_width)
    value_heads = values.reshape(req_local, nodes, local_heads, value_width)
    reached = ancestors(parents)
    scaled = jnp.einsum(
        "rihf,rjhf->rhij", query_heads, key_heads, preferred_element_type=jnp.float32
    ) / math.sqrt(feat_width)
    kernel = (1.0 + scaled + 0.5 * scaled * scaled) * reached[:, None, :, :]
    tree_den = jnp.transpose(jnp.sum(kernel, axis=-1), (0, 2, 1))
    tree_num = jnp.einsum(
        "rhij,rjhd->rihd",
        kernel.astype(jnp.bfloat16),
        value_heads,
        preferred_element_type=jnp.float32,
    )
    homes = page_home[:, 0]
    packer, packed_ids = pack_slots(homes, page_request, col_count, capacity)
    request_ids = jnp.arange(req_local, dtype=jnp.float32)
    sent_states = jnp.einsum(
        "ps,shfd->phfd",
        packer.astype(jnp.bfloat16),
        page_states,
        preferred_element_type=jnp.float32,
    ).astype(jnp.bfloat16)
    sent_norms = jnp.einsum("ps,shf->phf", packer, page_norms, precision=highest)
    got_states = lax.all_to_all(sent_states, "col", split_axis=0, concat_axis=0, tiled=True)
    got_norms, got_ids = (
        lax.all_to_all(
            sent_norms.astype(jnp.bfloat16), "col", split_axis=0, concat_axis=0, tiled=True
        ).astype(sent_norms.dtype),
        lax.all_to_all(
            packed_ids.astype(jnp.bfloat16), "col", split_axis=0, concat_axis=0, tiled=True
        ).astype(packed_ids.dtype),
    )
    unpack = (got_ids[None, :] == request_ids[:, None]).astype(jnp.float32)
    phi_query = feature_map(query_heads.astype(jnp.float32))
    phi_select = jnp.einsum(
        "rp,rnhf->pnhf",
        unpack.astype(jnp.bfloat16),
        phi_query.astype(jnp.bfloat16),
        preferred_element_type=jnp.float32,
    ).astype(jnp.bfloat16)
    phi_full = jnp.einsum("rp,rnhf->pnhf", unpack, phi_query, precision=highest)
    slot_num = jnp.einsum(
        "pnhf,phfd->pnhd", phi_select, got_states, preferred_element_type=jnp.float32
    )
    slot_den = jnp.einsum("pnhf,phf->pnh", phi_full, got_norms, precision=highest)
    pref_num = jnp.einsum("rp,pnhd->rnhd", unpack, slot_num, precision=highest)
    pref_den = jnp.einsum("rp,pnh->rnh", unpack, slot_den, precision=highest)
    mixed = ((pref_num + tree_num) / (pref_den + tree_den)[..., None]).astype(jnp.bfloat16)
    mixed = mixed.reshape(tok_local, local_heads * value_width)
    partial_value = jnp.dot(mixed, w_out, preferred_element_type=jnp.float32)
    feature_count = partial_value.shape[1]
    share = feature_count // row_count
    attn_all = lax.psum(partial_value.astype(jnp.bfloat16), "row").astype(jnp.float32)
    residual_all = hidden + attn_all
    normed_mlp = rms_norm(residual_all, mlp_gain).astype(jnp.bfloat16)
    residual = lax.dynamic_slice_in_dim(residual_all, row_index * share, share, 1)
    gate_proj = jnp.dot(normed_mlp, w_gate, preferred_element_type=jnp.float32)
    up_proj = jnp.dot(normed_mlp, w_up, preferred_element_type=jnp.float32)
    activated = (jax.nn.silu(gate_proj) * up_proj).astype(jnp.bfloat16)
    mlp_share = lax.psum_scatter(
        jnp.einsum("fd,tf->dt", w_down, activated, preferred_element_type=jnp.float32).astype(
            jnp.bfloat16
        ),
        "row",
        scatter_dimension=0,
        tiled=True,
    ).astype(jnp.float32)
    hidden_out = (residual + jnp.transpose(mlp_share)).astype(jnp.bfloat16)
    node_ids = jnp.arange(nodes, dtype=jnp.int32)
    chosen = (node_ids[None, :] == accepted[:, None]).astype(jnp.float32)
    path_mask = jnp.einsum("ri,rij->rj", chosen, reached, precision=highest)
    phi_key = feature_map(key_heads.astype(jnp.float32))
    new_norms = jnp.einsum("rj,rjhf->rhf", path_mask, phi_key, precision=highest)
    weighted = phi_key.astype(jnp.bfloat16) * path_mask.astype(jnp.bfloat16)[:, :, None, None]
    new_states = jnp.einsum(
        "rjhf,rjhd->rhfd", weighted, value_heads, preferred_element_type=jnp.float32
    ).astype(jnp.bfloat16)
    return (hidden_out, new_states, new_norms)


def solution(mesh):
    return jax.shard_map(
        local,
        mesh=mesh,
        in_specs=(
            P("col", "row"),
            P(),
            P(),
            P(None, "row"),
            P(None, "row"),
            P(None, "row"),
            P("row", None),
            P(None, "row"),
            P(None, "row"),
            P("row", None),
            P("col", "row", None, None),
            P("col", "row", None),
            P("col", None),
            P("col"),
            P("col", None),
            P("col"),
        ),
        out_specs=(P("col", "row"), P("col", "row", None, None), P("col", "row", None)),
        check_vma=False,
    )
```

profile of v0, /device:TPU:0, one launch (start us, length us, event | category | flops | bytes accessed | tf_op | source)
XLA Modules:
  0.0 250.5 jit_solution(17371456334453559667)
XLA Ops:
  7.2 1.0 convert_reduce_fusion
  8.2 0.7 multiply_add_fusion
  8.8 0.8 fusion.25
  9.7 0.7 all_to_all.16
  10.4 5.2 %all-to-all-start = ((bf16[8,4,1]{1,2,0:T(2,128)(2,1)}), bf16[8,4,1]{1,2,0:T(2,128)(2,1)S(1)}, u32[]{:S(2)}, u32[]{:S(2)}) async-start(bf16[8,4,1]{1,2,0:T(2,128)(2,1)} %all_to_all.16), calls=%async_computation | async-start | bytes 8192 | tf_op jit(solution)/shard_map/all_to_all | solution.py:117
  15.6 1.2 convolution_convert_fusion.6
  16.8 0.7 copy.217
  17.5 2.7 %all-to-all-done = bf16[8,4,1]{1,2,0:T(2,128)(2,1)S(1)} async-done(((bf16[8,4,1]{1,2,0:T(2,128)(2,1)}), bf16[8,4,1]{1,2,0:T(2,128)(2,1)S(1)}, u32[]{:S(2)}, u32[]{:S(2)}) %all-to-all-start) | async-done | bytes 96 | tf_op jit(solution)/shard_map/all_to_all | solution.py:117
  20.1 3.4 %all-to-all-start.2 = ((bf16[32,4,273]{2,1,0:T(4,128)(2,1)}), bf16[32,4,273]{2,1,0:T(4,128)(2,1)S(1)}, u32[]{:S(2)}, u32[]{:S(2)}) async-start(bf16[32,4,273]{2,1,0:T(4,128)(2,1)} %copy.217), calls=%async_computation.2 | async-start | bytes 196608 | tf_op jit(solution)/shard_map/all_to_all | solution.py:114
  23.5 4.9 %convolution_convert_fusion = bf16[32,4,273,112]{3,0,2,1:T(8,128)(2,1)S(1)} fusion(bf16[16,4,273,112]{3,1,2,0:T(4,128)(2,1)} %param.26, s32[16]{0:T(128)S(1)} %multiply_add_fusion), kind=kOutput, calls=%fused_computation.5 | convolution fusion | flops 129154560 | bytes 11741248 | tf_op jit(solution)/shard_map/ps,shfd->phfd/dot_general | solution.py:105
  28.4 10.4 %copy.202 = bf16[32,4,273,112]{3,1,2,0:T(4,128)(2,1)} copy(bf16[32,4,273,112]{3,0,2,1:T(8,128)(2,1)S(1)} %convolution_convert_fusion) | data formatting | bytes 15654912 | tf_op jit(solution)/shard_map/convert_element_type | solution.py:110
  38.7 0.6 copy-done.2
  39.4 5.0 %all-to-all-start.1 = ((bf16[32,4,273,112]{3,1,2,0:T(4,128)(2,1)}), bf16[32,4,273,112]{3,1,2,0:T(4,128)(2,1)}, u32[]{:S(2)}, u32[]{:S(2)}) async-start(bf16[32,4,273,112]{3,1,2,0:T(4,128)(2,1)} %copy.202), calls=%async_computation.1 | async-start | bytes 17891328 | tf_op jit(solution)/shard_map/all_to_all | solution.py:112
  44.4 0.0 all-reduce.2.cloned.1.call-start
  44.5 16.6 %all_gather.3 = bf16[128,1792]{0,1:T(8,128)(2,1)} all-gather(bf16[128,448]{0,1:T(8,128)(2,1)S(1)} %copy-done.8), channel_id=1, replica_groups=mesh['row'=4,'col'=8] {'row'}, dimensions={1}, use_global_device_ids=true | all-gather | bytes 573440 | tf_op jit(solution)/shard_map/all_gather | solution.py:81
  61.0 2.0 copy.199
  63.0 1.2 fusion.26
  64.2 1.4 convolution_convert_fusion.8
  65.7 0.1 reshape.103
  65.8 1.1 multiply_multiply_fusion.1
  66.9 2.4 copy.205
  69.3 0.2 copy.204
  69.5 1.4 convolution_convert_fusion.7
  71.0 0.7 reshape.105
  71.7 0.2 convolution_minimum_fusion.5
  71.9 0.2 convolution_minimum_fusion.4
  72.1 0.2 convolution_minimum_fusion.3
  72.3 0.2 convolution_minimum_fusion.2
  72.5 0.2 convolution_minimum_fusion.1
  72.7 0.2 convolution_minimum_fusion
  72.9 0.7 copy.212
  73.6 2.9 %convolution_convert_fusion.5 = bf16[128,448]{0,1:T(8,128)(2,1)} fusion(bf16[1792,448]{0,1:T(8,128)(2,1)} %param.21, bf16[128,1792]{1,0:T(8,128)(2,1)} %copy.199, f32[1792]{0:T(1024)S(1)} %copy-done.10, f32[128]{0:T(128)} %copy-done.13), kind=kOutput, calls=%fused_computation.23 | convolution fusion | flops 206495744 | bytes 2186752 | tf_op jit(solution)/shard_map/dot_general | solution.py:86
  76.5 1.7 reshape.123
  78.2 1.7 copy.213
  80.0 1.2 fusion.89
  81.1 1.8 fusion.45
  83.0 0.1 reshape.107
  83.1 5.9 %convolution_convert_fusion.1 = bf16[32,64,4,273]{3,0,2,1:T(8,128)(2,1)} fusion(f32[2,64,4,256]{3,0,2,1:T(2,128)} %copy.205, f32[2,64,4,16]{3,0,2,1:T(2,128)S(1)} %copy.204, f32[273]{0:T(512)S(1)} %pad.3.clone, f32[32]{0:T(128)S(1)} %reshape.107), kind=kOutput, calls=%fused_computation.9 | convolution fusion | flops 12020928 | bytes 5031108 | tf_op jit(solution)/shard_map/rp,rnhf->pnhf/dot_general | solution.py:123
  89.0 6.9 %fusion.52 = f32[32,64,4,273]{3,0,2,1:T(8,128)S(1)} fusion(f32[2,64,4,256]{3,0,2,1:T(2,128)S(1)} %copy-done.1, f32[2,64,4,16]{3,0,2,1:T(2,128)S(1)} %copy.204, f32[273]{0:T(512)S(1)} %pad.3.clone, f32[32]{0:T(128)S(1)} %reshape.107), kind=kOutput, calls=%fused_computation.70 | convolution fusion | flops 53953600 | bytes 9503940 | tf_op jit(solution)/shard_map/rp,rnhf->pnhf/dot_general | solution.py:129
  96.0 16.1 %fusion = f32[32,4,1,64]{3,2,1,0:T(1,128)S(1)} fusion(f32[32,64,4,273]{3,0,2,1:T(8,128)S(1)} %fusion.52, bf16[32,4,273,1]{2,1,0,3:T(4,128)(2,1)S(1)} %bitcast.101), kind=kOutput, calls=%fused_computation | convolution fusion | flops 26836992 | bytes 9048320 | tf_op jit(solution)/shard_map/pnhf,phf->pnh/dot_general | solution.py:133
  112.0 0.2 convolution_add_fusion
  112.2 0.8 copy.219
  113.0 31.5 %all-to-all-done.1 = bf16[32,4,273,112]{3,1,2,0:T(4,128)(2,1)} async-done(((bf16[32,4,273,112]{3,1,2,0:T(4,128)(2,1)}), bf16[32,4,273,112]{3,1,2,0:T(4,128)(2,1)}, u32[]{:S(2)}, u32[]{:S(2)}) %all-to-all-start.1) | async-done | bytes 7827488 | tf_op jit(solution)/shard_map/all_to_all | solution.py:112
  144.5 15.3 %fusion.9 = f32[32,64,4,112]{3,1,2,0:T(8,128)} fusion(bf16[32,64,4,273]{3,0,2,1:T(8,128)(2,1)} %convolution_convert_fusion.1, bf16[32,4,273,112]{3,1,2,0:T(4,128)(2,1)} %all-to-all-done.1), kind=kOutput, calls=%fused_computation.13 | convolution fusion | flops 500957184 | bytes 15970304 | tf_op jit(solution)/shard_map/pnhf,phfd->pnhd/dot_general | solution.py:130
  159.7 7.4 %fusion.21 = bf16[2,64,4,112]{3,0,2,1:T(2,128)(2,1)S(1)} fusion(f32[32,64,4,112]{3,1,2,0:T(8,128)} %fusion.9, f32[2,4,112,64]{2,3,1,0:T(8,128)S(1)} %copy-done.7, f32[2,64,4]{0,2,1:T(4,128)} %copy.219, f32[32]{0:T(128)S(1)} %reshape.107), kind=kOutput, calls=%fused_computation.22 | convolution fusion | flops 22192192 | bytes 4016256 | tf_op jit(solution)/shard_map/rp,pnhd->rnhd/dot_general | solution.py:134
  167.2 0.1 reshape.106
  167.4 2.6 %convolution_convert_fusion.3 = bf16[128,1792]{1,0:T(8,128)(2,1)} fusion(bf16[128,448]{1,0:T(8,128)(2,1)S(1)} %reshape.106, bf16[448,1792]{1,0:T(8,128)(2,1)} %param.22), kind=kOutput, calls=%fused_computation.11 | convolution fusion | flops 205750272 | bytes 2179072 | tf_op jit(solution)/shard_map/dot_general | solution.py:138
  170.1 0.1 compare_bitcast_fusion
  170.1 0.1 fusion.65
  170.3 0.8 copy_convert_fusion
  171.0 36.0 %all-reduce.2.cloned.1.call-done = bf16[128,1792]{1,0:T(8,128)(2,1)} async-done(((bf16[128,1792]{1,0:T(8,128)(2,1)}), bf16[128,1792]{1,0:T(8,128)(2,1)}) %all-reduce.2.cloned.1.call-update) | async-done | bytes 458768 | tf_op jit(solution)/shard_map/psum | solution.py:141
  207.0 2.2 convert_add_fusion
  209.3 3.7 %fusion.85 = f32[128,896]{1,0:T(8,128)} fusion(bf16[1792,896]{1,0:T(8,128)(2,1)} %param.23, f32[1792]{0:T(1024)S(1)} %copy-done.9, f32[128]{0:T(128)S(1)} %add_rsqrt_fusion, bf16[128,1792]{1,0:T(8,128)(2,1)} %copy.199, bf16[128,1792]{1,0:T(8,128)(2,1)} %all-reduce.2.cloned.1.call-done), kind=kOutput, calls=%fused_computation.118 | convolution fusion | flops 412418048 | bytes 4595200 | tf_op jit(solution)/shard_map/dot_general | solution.py:145
  213.0 4.4 %fusion.8 = bf16[1792,128]{0,1:T(8,128)(2,1)} fusion(bf16[896,1792]{1,0:T(8,128)(2,1)S(1)} %copy-done, bf16[1792,896]{1,0:T(8,128)(2,1)} %param.24, f32[128,896]{1,0:T(8,128)} %fusion.85, f32[1792]{0:T(1024)S(1)} %copy-done.9, f32[128]{0:T(128)S(1)} %add_rsqrt_fusion, bf16[128,1792]{1,0:T(8,128)(2,1)} %copy.199, ...), kind=kOutput, calls=%fused_computation.12 | convolution fusion | flops 824377344 | bytes 8265216 | tf_op jit(solution)/shard_map/fd,tf->dt/dot_general | solution.py:149
  217.3 2.0 copy.239
  219.4 0.1 multiply_multiply_fusion
  219.5 0.6 convolution_convert_fusion.4
  220.1 1.0 copy.226
  221.2 1.5 fusion.29
  222.7 0.6 copy.290
  223.3 17.1 %reduce-scatter.4.cloned.1.call-done = bf16[448,128]{1,0:T(8,128)(2,1)} async-done(((bf16[1792,128]{1,0:T(8,128)(2,1)}), bf16[448,128]{1,0:T(8,128)(2,1)}) %reduce-scatter.4.cloned.1.call-update) | async-done | bytes 114704
  240.4 1.0 copy.240
  241.4 1.1 fusion.42
  242.5 0.8 copy.225
  (41 shorter events, 0.3 us)
Async XLA Ops:
  7.2 205.8 %copy-start = (bf16[896,1792]{1,0:T(8,128)(2,1)S(1)}, bf16[896,1792]{1,0:T(8,128)(2,1)}, u32[]{:S(2)}) copy-start(bf16[896,1792]{1,0:T(8,128)(2,1)} %param.25) | copy-start | bytes 9633796
  10.4 9.8 %all-to-all-start = ((bf16[8,4,1]{1,2,0:T(2,128)(2,1)}), bf16[8,4,1]{1,2,0:T(2,128)(2,1)S(1)}, u32[]{:S(2)}, u32[]{:S(2)}) async-start(bf16[8,4,1]{1,2,0:T(2,128)(2,1)} %all_to_all.16), calls=%async_computation | async-start | bytes 8192 | tf_op jit(solution)/shard_map/all_to_all | solution.py:117
  20.1 18.6 %all-to-all-start.2 = ((bf16[32,4,273]{2,1,0:T(4,128)(2,1)}), bf16[32,4,273]{2,1,0:T(4,128)(2,1)S(1)}, u32[]{:S(2)}, u32[]{:S(2)}) async-start(bf16[32,4,273]{2,1,0:T(4,128)(2,1)} %copy.217), calls=%async_computation.2 | async-start | bytes 196608 | tf_op jit(solution)/shard_map/all_to_all | solution.py:114
  38.7 5.7 %copy-start.8 = (bf16[128,448]{0,1:T(8,128)(2,1)S(1)}, bf16[128,448]{0,1:T(8,128)(2,1)}, u32[]{:S(2)}) copy-start(bf16[128,448]{0,1:T(8,128)(2,1)} %param.16) | copy-start | bytes 344068
  38.7 25.5 %copy-start.10 = (f32[1792]{0:T(1024)S(1)}, f32[1792]{0:T(1024)}, u32[]{:S(2)}) copy-start(f32[1792]{0:T(1024)} %param.17) | copy-start | bytes 21508
  38.7 0.7 copy-start.2
  39.4 105.1 %all-to-all-start.1 = ((bf16[32,4,273,112]{3,1,2,0:T(4,128)(2,1)}), bf16[32,4,273,112]{3,1,2,0:T(4,128)(2,1)}, u32[]{:S(2)}, u32[]{:S(2)}) async-start(bf16[32,4,273,112]{3,1,2,0:T(4,128)(2,1)} %copy.202), calls=%async_computation.1 | async-start | bytes 17891328 | tf_op jit(solution)/shard_map/all_to_all | solution.py:112
  44.4 162.6 %all-reduce.2.cloned.1.call-start = ((), (), s32[]{:S(2)}) async-start(), calls=%async_computation.4 | async-start | bytes 917504 | tf_op jit(solution)/shard_map/psum | solution.py:141
  61.0 10.6 %copy-start.11 = (s32[2,64]{1,0:T(2,128)S(1)}, s32[2,64]{1,0:T(2,128)}, u32[]{:S(2)}) copy-start(s32[2,64]{1,0:T(2,128)} %param.30) | copy-start | bytes 1540
  64.2 5.1 %copy-start.13 = (f32[128]{0:T(128)}, f32[128]{0:T(128)S(1)}, u32[]{:S(2)}) copy-start(f32[128]{0:T(128)S(1)} %add_rsqrt_fusion.1) | copy-start | bytes 1540
  65.8 3.5 %copy-start.6 = (bf16[2,64,4,16]{1,0,3,2:T(2,128)(2,1)}, bf16[2,64,4,16]{1,0,3,2:T(2,128)(2,1)S(1)}, u32[]{:S(2)}) copy-start(bf16[2,64,4,16]{1,0,3,2:T(2,128)(2,1)S(1)} %reshape.103) | copy-start | bytes 49156
  83.1 6.0 %copy-start.1 = (f32[2,64,4,256]{3,0,2,1:T(2,128)S(1)}, f32[2,64,4,256]{3,0,2,1:T(2,128)}, u32[]{:S(2)}) copy-start(f32[2,64,4,256]{3,0,2,1:T(2,128)} %copy.205) | copy-start | bytes 1572868
  89.0 6.9 %copy-start.3 = (bf16[32,4,273]{2,1,0:T(4,128)(2,1)S(1)}, bf16[32,4,273]{2,1,0:T(4,128)(2,1)}, u32[]{:S(2)}) copy-start(bf16[32,4,273]{2,1,0:T(4,128)(2,1)} %copy-done.2) | copy-start | bytes 209668
  113.0 46.8 %copy-start.7 = (f32[2,4,112,64]{2,3,1,0:T(8,128)S(1)}, f32[2,4,112,64]{2,3,1,0:T(8,128)}, u32[]{:S(2)}) copy-start(f32[2,4,112,64]{2,3,1,0:T(8,128)} %fusion.45) | copy-start | bytes 688132
  159.7 10.3 %copy-start.12 = (s32[2]{0:T(128)S(1)}, s32[2]{0:T(128)}, u32[]{:S(2)}) copy-start(s32[2]{0:T(128)} %param.31) | copy-start | bytes 28
  167.2 42.1 %copy-start.9 = (f32[1792]{0:T(1024)S(1)}, f32[1792]{0:T(1024)}, u32[]{:S(2)}) copy-start(f32[1792]{0:T(1024)} %param.18) | copy-start | bytes 21508
  170.0 70.4 %reduce-scatter.4.cloned.1.call-start = ((), (), s32[]{:S(2)}) async-start(), calls=%async_computation.5 | async-start | bytes 573440
  213.0 6.4 %copy-start.5 = (bf16[2,64,4,16]{1,0,3,2:T(2,128)(2,1)S(1)}, bf16[2,64,4,16]{1,0,3,2:T(2,128)(2,1)}, u32[]{:S(2)}) copy-start(bf16[2,64,4,16]{1,0,3,2:T(2,128)(2,1)} %reshape.105) | copy-start | bytes 49156
  213.0 6.6 %copy-start.4 = (bf16[2,64,4,112]{3,1,2,0:T(8,128)(2,1)S(1)}, bf16[2,64,4,112]{3,1,2,0:T(8,128)(2,1)}, u32[]{:S(2)}) copy-start(bf16[2,64,4,112]{3,1,2,0:T(8,128)(2,1)} %copy.213) | copy-start | bytes 344068
Sparse Core Ops, SparseCore 0:
  170.1 36.8 all-reduce.1
  219.5 20.8 reduce-scatter.3
where the time goes:
time: 255 us; the launch traced here: 251 us
  waiting for transfers between devices  87.2 us (34%)
  matrix products  81.5 us (32%)
  local copies, waits for them, and re-layouts  28.5 us (11%)
  blocking collectives  16.6 us (7%)
  between operations  14.8 us (6%)
  starting transfers between devices  13.6 us (5%)
  other arithmetic  8.38 us (3%)
    psum x1, waiting for transfers between devices, local(): lax.psum(partial_value.astype(jnp.bfloat16), 'row').astype(jnp.float32)  36 us
    all_to_all x1, waiting for transfers between devices, local(): lax.all_to_all(sent_states, 'col', split_axis=0, concat_axis=0, tiled=True)  31.5 us
    unnamed x3, waiting for transfers between devices  17.1 us
    all_gather x1, blocking collectives, local(): gathered = lax.all_gather(hidden_in, 'row', axis=1, tiled=True)  16.6 us
    dot_general x1, matrix products, local(): jnp.einsum('pnhf,phf->pnh', phi_full, got_norms, precision=highest)  16.1 us
    dot_general x1, matrix products, local(): jnp.einsum('pnhf,phfd->pnhd', phi_select, got_states, preferred_element_t...  15.3 us
    convert_element_type x1, local copies, waits for them, and re-layouts, local(): sent_states = jnp.einsum('ps,shfd->phfd', packer.astype(jnp.bfloat16), pa...  10.4 us
    dot_general x1, matrix products, local(): pref_num = jnp.einsum('rp,pnhd->rnhd', unpack, slot_num, precision=highest)  7.43 us
  transfers between devices with their start and end apart: 5, of which 4 were waited for; matrix products, arithmetic and copies ran while one was open for 29% of the time, Pallas kernels for 0%

commit v1 on v0

--- a/solution.py
+++ b/solution.py
@@ -1,8 +1,12 @@
+import functools
 import math
 
 import jax
 import jax.numpy as jnp
+import numpy as np
 from jax import lax
+from jax.experimental import pallas as pl
+from jax.experimental.pallas import tpu as pltpu
 from jax.sharding import PartitionSpec as P
 
 epsilon = 1e-05
@@ -165,10 +169,485 @@
     ).astype(jnp.bfloat16)
     return (hidden_out, new_states, new_norms)
 
+MESH_KEYS = ("row", "col")
+
+
+def expansion(heads, feat_width, shifts, window):
+    count = heads * (1 + feat_width + feat_width * feat_width)
+    first = np.zeros((len(shifts), 128, window), np.float32)
+    second = np.zeros((len(shifts), 128, window), np.float32)
+    scale = np.zeros((len(shifts), 1, window), np.float32)
+    unit = heads * feat_width
+    for index, shift in enumerate(shifts):
+        for t in range(count):
+            f, h = divmod(t, heads)
+            column = shift + t
+            if f == 0:
+                a, b, c = unit + h, unit + h, 1.0
+            elif f <= feat_width:
+                a, b, c = h * feat_width + f - 1, unit + h, feat_width ** (-0.25)
+            else:
+                i, j = divmod(f - 1 - feat_width, feat_width)
+                a, b, c = h * feat_width + i, h * feat_width + j, (2.0 * feat_width) ** (-0.5)
+            first[index, a, column] = 1.0
+            second[index, b, column] = 1.0
+            scale[index, 0, column] = c
+    return first, second, scale
+
+
+def peers_of(axis):
+    size, me = lax.axis_size(axis), lax.axis_index(axis)
+    return [lax.rem(me + step, size) for step in range(1, size)]
+
+
+def greet():
+    barrier = pltpu.get_barrier_semaphore()
+    count = 0
+    for axis in MESH_KEYS:
+        for peer in peers_of(axis):
+            pl.semaphore_signal(
+                barrier, inc=1, device_id={axis: peer}, device_id_type=pl.DeviceIdType.MESH
+            )
+            count += 1
+    pl.semaphore_wait(barrier, count)
+
+
+def push(axis, source_of, target, send_sem, recv_sem):
+    copies = []
+    for step, peer in enumerate(peers_of(axis)):
+        copy = pltpu.make_async_remote_copy(
+            src_ref=source_of(peer),
+            dst_ref=target,
+            send_sem=send_sem.at[step],
+            recv_sem=recv_sem.at[step],
+            device_id={axis: peer},
+            device_id_type=pl.DeviceIdType.MESH,
+        )
+        copy.start()
+        copies.append(copy)
+    return copies
+
+
+def extended(rows_t, heads):
+    unit = rows_t.shape[0]
+    ids = lax.broadcasted_iota(jnp.int32, (128 - unit, rows_t.shape[1]), 0)
+    ones = jnp.where(ids < heads, 1.0, 0.0)
+    return jnp.concatenate([rows_t, ones], axis=0)
+
+
+def project_kernel(
+    heads, hidden_ref, gain_ref, wq_any, wk_any, wv_any,
+    hidden_out, q_out, qall_out, k_out, v_out,
+    wq, wk, wv, hid, normed, qext, qall, w_sem, hs_sem, hr_sem, qs_sem, qr_sem,
+):
+    me_row, me_col = lax.axis_index("row"), lax.axis_index("col")
+    share, tokens = hidden_ref.shape
+    loads = [
+        pltpu.make_async_copy(src, dst, w_sem.at[i])
+        for i, (src, dst) in enumerate(((wq_any, wq), (wk_any, wk), (wv_any, wv)))
+    ]
+    for load in loads:
+        load.start()
+    greet()
+    mine = hid.at[pl.ds(pl.multiple_of(me_row * share, 16), share)]
+    copies = push("row", lambda peer: hidden_ref, mine, hs_sem, hr_sem)
+    mine[...] = hidden_ref[...]
+    gain_t = jnp.transpose(gain_ref[...])
+    for copy in copies:
+        copy.wait_recv()
+    width = hid.shape[0]
+    total = jnp.zeros((1, tokens), jnp.float32)
+    for j in range(width // 128):
+        x = hid[128 * j : 128 * j + 128, :].astype(jnp.float32)
+        total += jnp.sum(x * x, axis=0, keepdims=True)
+    inverse = lax.rsqrt(total / width + epsilon)
+    for j in range(width // 128):
+        x = hid[128 * j : 128 * j + 128, :].astype(jnp.float32)
+        normed[128 * j : 128 * j + 128, :] = (x * inverse * gain_t[:, j : j + 1]).astype(jnp.bfloat16)
+    for load in loads:
+        load.wait()
+    q_t = jnp.dot(wq[...], normed[...], preferred_element_type=jnp.float32)
+    q_t = q_t.astype(jnp.bfloat16).astype(jnp.float32)
+    qext[...] = jnp.transpose(extended(q_t, heads)).astype(jnp.bfloat16)
+    own = qall.at[pl.ds(pl.multiple_of(me_col * tokens, 16), tokens)]
+    q_copies = push("col", lambda peer: qext, own, qs_sem, qr_sem)
+    own[...] = qext[...]
+    q_out[...] = qext[...]
+    k_t = jnp.dot(wk[...], normed[...], preferred_element_type=jnp.float32)
+    k_out[...] = extended(k_t, heads).astype(jnp.bfloat16)
+    v_t = jnp.dot(wv[...], normed[...], preferred_element_type=jnp.float32)
+    v_out[...] = v_t.astype(jnp.bfloat16)
+    hidden_out[...] = hid[...]
+    for copy in copies:
+        copy.wait_send()
+    for copy in q_copies:
+        copy.wait()
+    qall_out[...] = qall[...]
+
+
+def pages_kernel(
+    heads, nodes, shifts, starts, owner_ref, qall_ref, states_ref, norms_ref,
+    first_ref, second_ref, scale_ref, out_ref, total,
+):
+    step = pl.program_id(0)
+    window = first_ref.shape[2]
+    value_width = states_ref.shape[1]
+    span = heads * nodes
+
+    @pl.when(step == 0)
+    def clear():
+        total[...] = jnp.zeros_like(total)
+
+    cuts = [(lo, min(lo + 384, window)) for lo in range(0, window, 384)]
+    for i in range(len(shifts)):
+        owner = owner_ref[step * len(shifts) + i]
+        rows = qall_ref[pl.ds(pl.multiple_of(owner * nodes, 16), nodes), :]
+        num = jnp.zeros((span, value_width), jnp.float32)
+        weigh = jnp.zeros((nodes, 128), jnp.float32)
+        for lo, hi in cuts:
+            a = jnp.dot(rows, first_ref[i, :, lo:hi], preferred_element_type=jnp.float32)
+            b = jnp.dot(rows, second_ref[i, :, lo:hi], preferred_element_type=jnp.float32)
+            phi = a * b * scale_ref[i, :, lo:hi]
+            weighted = phi * norms_ref[0, i : i + 1, lo:hi]
+            for at in range(0, hi - lo, 128):
+                part = weighted[:, at : min(at + 128, hi - lo)]
+                if part.shape[1] < 128:
+                    part = jnp.concatenate(
+                        [part, jnp.zeros((nodes, 128 - part.shape[1]), jnp.float32)], axis=1
+                    )
+                weigh += part
+            head_of = lax.broadcasted_iota(jnp.int32, phi.shape, 1) % heads
+            masked = jnp.concatenate(
+                [jnp.where(head_of == h, phi, 0.0).astype(jnp.bfloat16) for h in range(heads)], axis=0
+            )
+            num += jnp.dot(
+                masked, states_ref[starts[i] + lo : starts[i] + hi, :], preferred_element_type=jnp.float32
+            )
+        lane_head = lax.broadcasted_iota(jnp.int32, weigh.shape, 1) % heads
+        den = jnp.concatenate(
+            [
+                jnp.sum(jnp.where(lane_head == h, weigh, 0.0), axis=1, keepdims=True)
+                for h in range(heads)
+            ],
+            axis=0,
+        )
+        at = pl.ds(pl.multiple_of(owner * span, 16), span)
+        total[at, 0:value_width] += num
+        total[at, value_width : value_width + 1] += den
+
+    @pl.when(step == pl.num_programs(0) - 1)
+    def finish():
+        out_ref[...] = total[...].astype(jnp.bfloat16)
+
+
+def layer_kernel(
+    heads, feat_width, value_width, requests,
+    pref_any, hidden_ref, q_ref, k_ref, v_ref, parent_ref, chosen_ref, gain_ref, first_ref, second_ref,
+    wout_any, wgate_any, wup_any, wdown_any,
+    out_ref, states_out, norms_out,
+    prefs, wout, wgate, wup, wdown, hid, stacked, sums, parts, gathered, blocks, kept, arrived,
+    w_sem, own_sem, ps_sem, pr_sem, as_sem, ar_sem, gs_sem, gr_sem, ms_sem, mr_sem,
+):
+    me_row, me_col = lax.axis_index("row"), lax.axis_index("col")
+    row_count = lax.axis_size("row")
+    tokens, width = hid.shape
+    nodes = tokens // requests
+    span = requests * heads * nodes
+    unit = heads * feat_width
+    loads = [
+        pltpu.make_async_copy(src, dst, w_sem.at[i])
+        for i, (src, dst) in enumerate(
+            ((wout_any, wout), (wgate_any, wgate), (wup_any, wup), (wdown_any, wdown))
+        )
+    ]
+    for load in loads:
+        load.start()
+    greet()
+    block_of = lambda home: pref_any.at[pl.ds(pl.multiple_of(home * span, 16), span)]
+    pref_copies = push("col", block_of, prefs.at[me_col], ps_sem, pr_sem)
+    own = pltpu.make_async_copy(block_of(me_col), prefs.at[me_col], own_sem)
+    own.start()
+
+    row_ids = lax.broadcasted_iota(jnp.int32, (tokens, tokens), 0)
+    lane_ids = lax.broadcasted_iota(jnp.int32, (tokens, tokens), 1)
+    linked = jnp.logical_or(parent_ref[...] == lane_ids, row_ids == lane_ids)
+    reached = jnp.where(linked, 1.0, 0.0)
+    for repeat in range(max(1, (nodes - 1).bit_length())):
+        low = reached.astype(jnp.bfloat16)
+        reached = jnp.minimum(jnp.dot(low, low, preferred_element_type=jnp.float32), 1.0)
+
+    for j in range(width // 128):
+        block = hidden_ref[128 * j : 128 * j + 128, :].astype(jnp.float32)
+        hid[:, 128 * j : 128 * j + 128] = jnp.transpose(block)
+
+    tree_num, tree_den = [], []
+    q = q_ref[...]
+    q_lane = lax.broadcasted_iota(jnp.int32, q.shape, 1)
+    for h in range(heads):
+        mine = jnp.logical_and(q_lane >= h * feat_width, q_lane < (h + 1) * feat_width)
+        q_head = jnp.where(mine, q.astype(jnp.float32), 0.0).astype(jnp.bfloat16)
+        scaled = jnp.dot(q_head, k_ref[...], preferred_element_type=jnp.float32) / math.sqrt(feat_width)
+        kernel = (1.0 + scaled + 0.5 * scaled * scaled) * reached
+        tree_den.append(jnp.sum(kernel, axis=1, keepdims=True))
+        tree_num.append(
+            lax.dot_general(
+                kernel.astype(jnp.bfloat16),
+                v_ref[h * value_width : (h + 1) * value_width, :],
+                (((1,), (1,)), ((), ())),
+                preferred_element_type=jnp.float32,
+            )
+        )
+
+    path = jnp.dot(chosen_ref[...], reached.astype(jnp.bfloat16), preferred_element_type=jnp.float32)
+    a = jnp.dot(first_ref[...], k_ref[...], preferred_element_type=jnp.float32)
+    b = jnp.dot(second_ref[...], k_ref[...], preferred_element_type=jnp.float32)
+    t = lax.broadcasted_iota(jnp.int32, a.shape, 0)
+    scale = jnp.where(
+        t < heads,
+        1.0,
+        jnp.where(t < heads * (1 + feat_width), feat_width ** (-0.25), (2.0 * feat_width) ** (-0.5)),
+    )
+    phi = a * b * scale
+    high = phi.astype(jnp.bfloat16)
+    rest = (phi - high.astype(jnp.float32)).astype(jnp.bfloat16)
+    across = (((1,), (1,)), ((), ()))
+    path_low = path.astype(jnp.bfloat16)
+    norms_out[...] = lax.dot_general(
+        path_low, high, across, preferred_element_type=jnp.float32
+    ) + lax.dot_general(path_low, rest, across, preferred_element_type=jnp.float32)
+    for h in range(heads):
+        stacked[h * tokens : (h + 1) * tokens, :] = jnp.transpose(
+            v_ref[h * value_width : (h + 1) * value_width, :].astype(jnp.float32)
+        ).astype(jnp.bfloat16)
+    count = states_out.shape[0] // requests
+    high_full = high.astype(jnp.float32)
+    for r in range(requests):
+        weighted = high_full * path[r : r + 1, :]
+        wide = jnp.concatenate(
+            [jnp.where(t % heads == h, weighted, 0.0).astype(jnp.bfloat16) for h in range(heads)], axis=1
+        )
+        page = jnp.dot(wide, stacked[...], preferred_element_type=jnp.float32)
+        states_out[r * count : (r + 1) * count, :] = page[0:count, :].astype(jnp.bfloat16)
+
+    own.wait()
+    for copy in pref_copies:
+        copy.wait()
+    pref = prefs[0].astype(jnp.float32)
+    for s in range(1, prefs.shape[0]):
+        pref += prefs[s].astype(jnp.float32)
+    loads[0].wait()
+    partial = jnp.zeros((tokens, width), jnp.float32)
+    for h in range(heads):
+        rows = jnp.concatenate(
+            [pref[(r * heads + h) * nodes : (r * heads + h + 1) * nodes, :] for r in range(requests)], axis=0
+        )
+        num = rows[:, 0:value_width] + tree_num[h]
+        den = rows[:, value_width : value_width + 1] + tree_den[h]
+        mixed = (num / den).astype(jnp.bfloat16)
+        partial += jnp.dot(
+            mixed, wout[h * value_width : (h + 1) * value_width, :], preferred_element_type=jnp.float32
+        )
+    sums[...] = partial.astype(jnp.bfloat16)
+
+    share = tokens // row_count
+    rows_of = lambda row: pl.ds(pl.multiple_of(row * share, 16), share)
+    copies = push("row", lambda row: sums.at[rows_of(row)], parts.at[me_row], as_sem, ar_sem)
+    parts[me_row] = sums[rows_of(me_row), :]
+    for copy in copies:
+        copy.wait()
+    attn = parts[0].astype(jnp.float32)
+    for g in range(1, row_count):
+        attn += parts[g].astype(jnp.float32)
+    gathered[rows_of(me_row), :] = attn.astype(jnp.bfloat16)
+    mine = gathered.at[rows_of(me_row)]
+    copies = push("row", lambda row: mine, mine, gs_sem, gr_sem)
+    for copy in copies:
+        copy.wait()
+
+    residual = hid[...] + gathered[...].astype(jnp.float32)
+    feature_share = width // row_count
+    for g in range(row_count):
+        kept[g] = residual[:, g * feature_share : (g + 1) * feature_share]
+    inverse = lax.rsqrt(jnp.sum(residual * residual, axis=1, keepdims=True) / width + epsilon)
+    normed = (residual * inverse * gain_ref[...]).astype(jnp.bfloat16)
+    loads[1].wait()
+    gate = jnp.dot(normed, wgate[...], preferred_element_type=jnp.float32)
+    loads[2].wait()
+    up = jnp.dot(normed, wup[...], preferred_element_type=jnp.float32)
+    active = (gate / (1.0 + jnp.exp(-gate)) * up).astype(jnp.bfloat16)
+    loads[3].wait()
+    mlp = jnp.dot(active, wdown[...], preferred_element_type=jnp.float32)
+    for g in range(row_count):
+        blocks[g] = mlp[:, g * feature_share : (g + 1) * feature_share].astype(jnp.bfloat16)
+    copies = push("row", lambda row: blocks.at[row], arrived.at[me_row], ms_sem, mr_sem)
+    arrived[me_row] = blocks[me_row]
+    for copy in copies:
+        copy.wait()
+    final = kept[me_row]
+    for g in range(row_count):
+        final += arrived[g].astype(jnp.float32)
+    out_ref[...] = final.astype(jnp.bfloat16)
+
+
+def kernel_local(
+    hidden_in, attn_gain, mlp_gain, w_query, w_key, w_value, w_out, w_gate, w_up, w_down,
+    page_states, page_norms, page_home, page_request, parents, accepted,
+):
+    slots, heads, features, value_width = page_states.shape
+    feat_width = w_query.shape[1] // heads
+    requests, nodes = parents.shape
+    tokens, share = hidden_in.shape
+    width, hidden_units = w_gate.shape
+    rows, cols = lax.axis_size("row"), lax.axis_size("col")
+    bf16, f32 = jnp.bfloat16, jnp.float32
+    vmem = pl.BlockSpec(memory_space=pltpu.VMEM)
+    hbm = pl.BlockSpec(memory_space=pl.ANY)
+    dma = pltpu.SemaphoreType.DMA
+    unit = heads * feat_width
+    limit = 56 * 1024 * 1024
+
+    hidden_t, q_own, q_all, k_t, v_t = pl.pallas_call(
+        functools.partial(project_kernel, heads),
+        out_shape=(
+            jax.ShapeDtypeStruct((width, tokens), bf16),
+            jax.ShapeDtypeStruct((tokens, 128), bf16),
+            jax.ShapeDtypeStruct((cols * tokens, 128), bf16),
+            jax.ShapeDtypeStruct((128, tokens), bf16),
+            jax.ShapeDtypeStruct((heads * value_width, tokens), bf16),
+        ),
+        in_specs=[vmem, vmem, hbm, hbm, hbm],
+        out_specs=(vmem,) * 5,
+        scratch_shapes=[
+            pltpu.VMEM((unit, width), bf16),
+            pltpu.VMEM((unit, width), bf16),
+            pltpu.VMEM((heads * value_width, width), bf16),
+            pltpu.VMEM((width, tokens), bf16),
+            pltpu.VMEM((width, tokens), bf16),
+            pltpu.VMEM((tokens, 128), bf16),
+            pltpu.VMEM((cols * tokens, 128), bf16),
+            dma((3,)),
+            dma((rows - 1,)),
+            dma((rows - 1,)),
+            dma((cols - 1,)),
+            dma((cols - 1,)),
+        ],
+        compiler_params=pltpu.CompilerParams(
+            collective_id=0, has_side_effects=True, vmem_limit_bytes=limit
+        ),
+        name="project",
+    )(hidden_in.T, attn_gain.reshape(width // 128, 128), w_query.T, w_key.T, w_value.T)
+
+    count = heads * features
+    group = 16 // math.gcd(count, 16)
+    shifts = [(count * i) % 16 for i in range(group)]
+    starts = [count * i - shifts[i] for i in range(group)]
+    window = -(-(count + max(shifts)) // 16) * 16
+    first, second, scale = expansion(heads, feat_width, shifts, window)
+    state_rows = jnp.transpose(page_states, (0, 2, 1, 3)).reshape(slots * count, value_width)
+    norm_rows = jnp.transpose(page_norms, (0, 2, 1)).reshape(slots // group, group, count)
+    norm_rows = jnp.stack(
+        [jnp.pad(norm_rows[:, i], ((0, 0), (s, window - count - s))) for i, s in enumerate(shifts)], axis=1
+    )
+    owner = (page_home[:, 0] * requests + page_request).astype(jnp.int32)
+    total_rows = cols * requests * heads * nodes
+    whole = lambda *shape: pl.BlockSpec(shape, lambda s, o: (0,) * len(shape))
+    pref = pl.pallas_call(
+        functools.partial(pages_kernel, heads, nodes, shifts, starts),
+        out_shape=jax.ShapeDtypeStruct((total_rows, 128), bf16),
+        grid_spec=pltpu.PrefetchScalarGridSpec(
+            num_scalar_prefetch=1,
+            grid=(slots // group,),
+            in_specs=[
+                whole(cols * tokens, 128),
+                pl.BlockSpec((group * count, value_width), lambda s, o: (s, 0)),
+                pl.BlockSpec((1, group, window), lambda s, o: (s, 0, 0)),
+                whole(group, 128, window),
+                whole(group, 128, window),
+                whole(group, 1, window),
+            ],
+            out_specs=whole(total_rows, 128),
+            scratch_shapes=[pltpu.VMEM((total_rows, 128), f32)],
+        ),
+        compiler_params=pltpu.CompilerParams(vmem_limit_bytes=limit),
+        name="pages",
+    )(owner, q_all, state_rows, norm_rows, jnp.asarray(first, bf16), jnp.asarray(second, bf16), jnp.asarray(scale))
+
+    parent_rows = (parents + nodes * jnp.arange(requests, dtype=jnp.int32)[:, None]).reshape(tokens, 1)
+    accepted_rows = accepted + nodes * jnp.arange(requests, dtype=jnp.int32)
+    chosen = jnp.arange(tokens, dtype=jnp.int32)[None, :] == accepted_rows[:, None]
+    chosen = jnp.pad(chosen.astype(bf16), ((0, 16 - requests), (0, 0)))
+    first_t = jnp.asarray(first[0].T, bf16)
+    second_t = jnp.asarray(second[0].T, bf16)
+    span = requests * heads * nodes
+    token_share = tokens // rows
+    hidden_out, state_out, norm_out = pl.pallas_call(
+        functools.partial(layer_kernel, heads, feat_width, value_width, requests),
+        out_shape=(
+            jax.ShapeDtypeStruct((tokens, share), bf16),
+            jax.ShapeDtypeStruct((requests * count, value_width), bf16),
+            jax.ShapeDtypeStruct((16, window), f32),
+        ),
+        in_specs=[hbm] + [vmem] * 9 + [hbm] * 4,
+        out_specs=(vmem,) * 3,
+        scratch_shapes=[
+            pltpu.VMEM((cols, span, 128), bf16),
+            pltpu.VMEM(w_out.shape, bf16),
+            pltpu.VMEM(w_gate.shape, bf16),
+            pltpu.VMEM(w_up.shape, bf16),
+            pltpu.VMEM(w_down.shape, bf16),
+            pltpu.VMEM((tokens, width), f32),
+            pltpu.VMEM((heads * tokens, value_width), bf16),
+            pltpu.VMEM((tokens, width), bf16),
+            pltpu.VMEM((rows, token_share, width), bf16),
+            pltpu.VMEM((tokens, width), bf16),
+            pltpu.VMEM((rows, tokens, share), bf16),
+            pltpu.VMEM((rows, tokens, share), f32),
+            pltpu.VMEM((rows, tokens, share), bf16),
+            dma((4,)),
+            dma,
+            dma((cols - 1,)),
+            dma((cols - 1,)),
+        ]
+        + [dma((rows - 1,))] * 6,
+        compiler_params=pltpu.CompilerParams(
+            collective_id=1, has_side_effects=True, vmem_limit_bytes=limit
+        ),
+        name="layer",
+    )(
+        pref, hidden_t, q_own, k_t, v_t, parent_rows, chosen, mlp_gain.reshape(1, width),
+        first_t, second_t, w_out, w_gate, w_up, w_down,
+    )
+    new_states = jnp.transpose(state_out.reshape(requests, features, heads, value_width), (0, 2, 1, 3))
+    new_norms = jnp.transpose(norm_out[:requests, :count].reshape(requests, features, heads), (0, 2, 1))
+    return (hidden_out, new_states, new_norms)
+
+
+def kernels_fit(*arrays):
+    hidden_in, w_query, page_states, parents = arrays[0], arrays[3], arrays[10], arrays[14]
+    slots, heads, features, value_width = page_states.shape
+    tokens, rows = hidden_in.shape[0], lax.axis_size("row")
+    group = 16 // math.gcd(heads * features, 16)
+    return (
+        tokens == 128
+        and tokens % (16 * rows) == 0
+        and hidden_in.shape[1] % 16 == 0
+        and 128 % heads == 0
+        and (group == 1 or 16 % heads == 0)
+        and w_query.shape[1] + heads <= 128
+        and value_width < 128
+        and value_width % 16 == 0
+        and slots % group == 0
+        and parents.shape[0] <= 16
+    )
+
+
+def on_device(*arrays):
+    return kernel_local(*arrays) if kernels_fit(*arrays) else local(*arrays)
+
 
 def solution(mesh):
     return jax.shard_map(
-        local,
+        on_device,
         mesh=mesh,
         in_specs=(
             P("col", "row"),

time: 255 us -> 102 us (0.40); the launches traced: 251 us -> 102 us
  Pallas kernels: 0 us -> 89.6 us
  waiting for transfers between devices: 87.2 us -> 0 us
  matrix products: 81.5 us -> 0 us
  local copies, waits for them, and re-layouts: 28.5 us -> 9.4 us
  blocking collectives: 16.6 us -> 0 us
  between operations: 14.8 us -> 0.77 us
  starting transfers between devices: 13.6 us -> 0 us
  other arithmetic: 8.38 us -> 1.98 us
    pallas_call x0 -> x3, Pallas kernels: none -> 89.6 us  [the longest x1 55.9 us: kernel_local(): pl.pallas_call(functools.partial(layer_kernel, heads, feat_width, value_w...]
    dot_general x26 -> x0, matrix products: 81.5 us -> none  [the longest x1 16.1 us: local(): jnp.einsum('pnhf,phf->pnh', phi_full, got_norms, precision=highest)]
    psum x1 -> x0, waiting for transfers between devices: 36 us -> none  [local(): lax.psum(partial_value.astype(jnp.bfloat16), 'row').astype(jnp.float32)]
    all_to_all x3 -> x0, waiting for transfers between devices: 34.1 us -> none  [the longest x1 31.5 us: local(): lax.all_to_all(sent_states, 'col', split_axis=0, concat_axis=0, tiled=True)]
    unnamed x3 -> x0, waiting for transfers between devices: 17.1 us -> none
    all_gather x1 -> x0, blocking collectives: 16.6 us -> none  [local(): gathered = lax.all_gather(hidden_in, 'row', axis=1, tiled=True)]
    all_to_all x3 -> x0, starting transfers between devices: 13.5 us -> none  [the longest x1 5.17 us: local(): lax.all_to_all(packed_ids.astype(jnp.bfloat16), 'col', split_axis=0, conc...]
    convert_element_type x4 -> x0, local copies, waits for them, and re-layouts: 11.2 us -> none  [the longest x1 10.4 us: local(): sent_states = jnp.einsum('ps,shfd->phfd', packer.astype(jnp.bfloat16), pa...]
  transfers between devices with their start and end apart: 5 -> 0, of which waited for: 4 -> 0; matrix products, arithmetic and copies ran while one was open for 29% -> 0% of each run, Pallas kernels for 0% -> 0%
where the time goes in v1:
time: 102 us
  Pallas kernels  89.6 us (88%)
  local copies, waits for them, and re-layouts  9.4 us (9%)
  other arithmetic  1.98 us (2%)
    pallas_call x1, Pallas kernels, kernel_local(): pl.pallas_call(functools.partial(layer_kernel, heads, feat_width, value_w...  55.9 us
    pallas_call x1, Pallas kernels, kernel_local(): pl.pallas_call(functools.partial(project_kernel, heads), out_shape=(jax.S...  21.3 us
    pallas_call x1, Pallas kernels, kernel_local(): pl.pallas_call(functools.partial(pages_kernel, heads, nodes, shifts, star...  12.3 us
    unnamed x13, local copies, waits for them, and re-layouts  4.49 us

profile of v1, /device:TPU:0, one launch (start us, length us, event | category | flops | bytes accessed | tf_op | source)
XLA Modules:
  0.0 101.8 jit_solution(7742217339273056309)
XLA Ops:
  0.6 1.6 %copy.30 = f32[16,273,4]{2,1,0:T(8,128)S(1)} copy(f32[16,273,4]{1,2,0:T(4,128)} %bitcast.30) | data formatting | bytes 139776 | tf_op jit(solution)/shard_map/transpose | solution.py:547
  2.2 0.0 copy-start.2
  2.2 0.0 copy-start.3
  2.2 0.6 reshape.37
  2.9 0.1 fusion.1
  3.0 0.1 pad.23
  3.1 0.1 pad.24
  3.2 0.1 pad.25
  3.3 0.7 pad_maximum_fusion.norms_ref
  4.0 21.3 %project.1 = (bf16[1792,128]{1,0:T(8,128)(2,1)}, bf16[128,128]{1,0:T(8,128)(2,1)}, bf16[1024,128]{1,0:T(8,128)(2,1)}, bf16[128,128]{1,0:T(8,128)(2,1)}, bf16[448,128]{1,0:T(8,128)(2,1)}) custom-call(bf16[448,128]{1,0:T(8,128)(2,1)} %bitcast.29, f32[14,128]{1,0:T(8,128)} %bitcast.31, bf16[64,1792]{1,0:T(8,128)(2,1)} %bitcast.27, bf16[64,1792]{1,0:T(8,128)(2,1)} %bitcast.28, ...), custom_call_target="tpu_custom_call" | custom-call | tf_op jit(solution)/shard_map/project/pallas_call | solution.py:509
  25.4 0.0 copy-done.2
  25.4 0.0 copy-done.3
  25.4 0.5 bitcast_add_fusion.owner_ref
  25.9 0.0 copy-start.1
  25.9 0.0 copy-start
  25.9 0.0 copy-start.4
  25.9 12.3 %pages.1.pref_any = bf16[4096,128]{1,0:T(8,128)(2,1)} custom-call(s32[16]{0:T(128)} %bitcast_add_fusion.owner_ref, bf16[1024,128]{1,0:T(8,128)(2,1)} %get-tuple-element.11.qall_ref, bf16[17472,112]{1,0:T(8,128)(2,1)} %bitcast.23, f32[4,4,1104]{2,1,0:T(4,128)} %pad_maximum_fusion.norms_ref, bf16[4,128,1104]{2,1,0:T(8,128)(2,1)} %constant.21.clone.first_ref, ...), custom_call_target="tpu_custom_call" | custom-call | tf_op jit(solution)/shard_map/pages/pallas_call | solution.py:554
  38.3 0.0 copy-done.1
  38.3 0.1 broadcast_add_fusion
  38.4 0.8 reshape.42.parent_ref
  39.1 0.0 copy-done
  39.1 0.6 reshape.39.gain_ref
  39.7 0.0 copy-done.4
  39.7 0.1 iota_compare_fusion
  39.8 0.6 pad_convert_fusion.chosen_ref
  40.4 55.9 %layer.1 = (bf16[128,448]{1,0:T(8,128)(2,1)}, bf16[2184,112]{1,0:T(8,128)(2,1)}, f32[16,1104]{1,0:T(8,128)}) custom-call(bf16[4096,128]{1,0:T(8,128)(2,1)} %pages.1.pref_any, bf16[1792,128]{1,0:T(8,128)(2,1)} %get-tuple-element.12.hidden_ref, bf16[128,128]{1,0:T(8,128)(2,1)} %get-tuple-element.13.q_ref, bf16[128,128]{1,0:T(8,128)(2,1)} %get-tuple-element.14.k_ref, ...), custom_call_target="tpu_custom_call" | custom-call | tf_op jit(solution)/shard_map/layer/pallas_call | solution.py:583
  96.4 0.8 slice.19
  97.1 0.2 reshape.41
  97.3 0.8 copy.37
  98.1 1.7 %copy.36 = bf16[128,448]{0,1:T(8,128)(2,1)} copy(bf16[128,448]{1,0:T(8,128)(2,1)} %get-tuple-element.22) | data formatting | bytes 229376
  99.7 2.0 %copy.47 = bf16[2,4,273,112]{3,1,2,0:T(4,128)(2,1)} copy(bf16[2,4,273,112]{3,1,2,0:T(4,128)(2,1)} %bitcast.26) | data formatting | bytes 978432
  (9 shorter events, 0.1 us)
Async XLA Ops:
  2.2 23.2 %copy-start.2 = (s32[16]{0:T(128)S(1)}, s32[16]{0:T(128)}, u32[]{:S(2)}) copy-start(s32[16]{0:T(128)} %param.34) | copy-start | bytes 196
  2.2 23.2 %copy-start.3 = (s32[16,1]{0,1:T(1,128)S(1)}, s32[16,1]{0,1:T(1,128)}, u32[]{:S(2)}) copy-start(s32[16,1]{0,1:T(1,128)} %param.33) | copy-start | bytes 196
  25.9 12.4 %copy-start.1 = (s32[2,64]{1,0:T(2,128)S(1)}, s32[2,64]{1,0:T(2,128)}, u32[]{:S(2)}) copy-start(s32[2,64]{1,0:T(2,128)} %param.35) | copy-start | bytes 1540
  25.9 13.2 %copy-start = (f32[1792]{0:T(1024)S(1)}, f32[1792]{0:T(1024)}, u32[]{:S(2)}) copy-start(f32[1792]{0:T(1024)} %param.23) | copy-start | bytes 21508
  25.9 13.8 %copy-start.4 = (s32[2]{0:T(128)S(1)}, s32[2]{0:T(128)}, u32[]{:S(2)}) copy-start(s32[2]{0:T(128)} %param.36) | copy-start | bytes 28

commit v2 on v0

--- a/solution.py
+++ b/solution.py
@@ -1,8 +1,12 @@
+import functools
 import math
 
 import jax
 import jax.numpy as jnp
+import numpy as np
 from jax import lax
+from jax.experimental import pallas as pl
+from jax.experimental.pallas import tpu as pltpu
 from jax.sharding import PartitionSpec as P
 
 epsilon = 1e-05
@@ -165,10 +169,496 @@
     ).astype(jnp.bfloat16)
     return (hidden_out, new_states, new_norms)
 
+MESH_KEYS = ("row", "col")
+
+
+def picks(heads, feat_width, order, length):
+    unit = heads * feat_width
+    first = np.zeros((length, 128), np.float32)
+    second = np.zeros((length, 128), np.float32)
+    for h in range(heads):
+        for f in range(1 + feat_width + feat_width * feat_width):
+            if f == 0:
+                a, b = unit + h, unit + h
+            elif f <= feat_width:
+                a, b = h * feat_width + f - 1, unit + h
+            else:
+                i, j = divmod(f - 1 - feat_width, feat_width)
+                a, b = h * feat_width + i, h * feat_width + j
+            first[order(f, h), a] = 1.0
+            second[order(f, h), b] = 1.0
+    return first, second
+
+
+def feature_scale(feature, feat_width):
+    square = (2.0 * feat_width) ** (-0.5)
+    linear = feat_width ** (-0.25)
+    return jnp.where(feature == 0, 1.0, jnp.where(feature <= feat_width, linear, square))
+
+
+def peers_of(axis):
+    size, me = lax.axis_size(axis), lax.axis_index(axis)
+    return [lax.rem(me + step, size) for step in range(1, size)]
+
+
+def greet():
+    barrier = pltpu.get_barrier_semaphore()
+    count = 0
+    for axis in MESH_KEYS:
+        for peer in peers_of(axis):
+            pl.semaphore_signal(
+                barrier, inc=1, device_id={axis: peer}, device_id_type=pl.DeviceIdType.MESH
+            )
+            count += 1
+    pl.semaphore_wait(barrier, count)
+
+
+def push(axis, peers, source_of, target, send_sem, recv_sem):
+    copies = []
+    for step, peer in enumerate(peers):
+        copy = pltpu.make_async_remote_copy(
+            src_ref=source_of(step, peer),
+            dst_ref=target,
+            send_sem=send_sem.at[step],
+            recv_sem=recv_sem.at[step],
+            device_id={axis: peer},
+            device_id_type=pl.DeviceIdType.MESH,
+        )
+        copy.start()
+        copies.append(copy)
+    return copies
+
+
+def extended(rows_t, heads):
+    unit, tokens = rows_t.shape
+    ids = lax.broadcasted_iota(jnp.int32, (128 - unit, tokens), 0)
+    ones = jnp.where(ids < heads, 1.0, 0.0).astype(jnp.bfloat16)
+    return jnp.concatenate([rows_t, ones], axis=0)
+
+
+def dot(a, b, contract=(1, 0)):
+    return lax.dot_general(
+        a, b, (((contract[0],), (contract[1],)), ((), ())), preferred_element_type=jnp.float32
+    )
+
+
+def layer_kernel(
+    heads, feat_width, features, value_width, requests, capacity,
+    plan_ref, hidden_ref, gain_ref, mlp_gain_ref, norms_ref, parent_ref, chosen_ref,
+    first_ref, second_ref, first_t_ref, second_t_ref, first_h_ref, second_h_ref,
+    wq_any, wk_any, wv_any, states_any, wout_any, wgate_any, wup_any, wdown_any,
+    out_ref, states_out, norms_out,
+    wq, wk, wv, states, wout, wgate, wup, wdown,
+    hid_t, normed, q_mine, q_all, k_mine, v_mine, spread, phi_all, nums,
+    pair_out, pair_in, chip_out, chip_in,
+    hid, stacked, sums, parts, gathered, blocks, kept, arrived,
+    w_sem, hs_sem, hr_sem, qs_sem, qr_sem, bs_sem, br_sem, cs_sem, cr_sem,
+    as_sem, ar_sem, gs_sem, gr_sem, ms_sem, mr_sem,
+):
+    bf16, f32 = jnp.bfloat16, jnp.float32
+    me_row, me_col = lax.axis_index("row"), lax.axis_index("col")
+    row_count, col_count = lax.axis_size("row"), lax.axis_size("col")
+    chips = col_count // 2
+    me_chip, me_core = me_col // 2, lax.rem(me_col, 2)
+    tokens, width = hid.shape
+    nodes = tokens // requests
+    unit = heads * feat_width
+    span = heads * nodes
+    count = heads * features
+    window = phi_all.shape[2]
+    slots = norms_ref.shape[0] // heads
+    loads = [
+        pltpu.make_async_copy(src, dst, w_sem.at[i])
+        for i, (src, dst) in enumerate(
+            (
+                (wq_any, wq), (wk_any, wk), (wv_any, wv), (states_any, states),
+                (wout_any, wout), (wgate_any, wgate), (wup_any, wup), (wdown_any, wdown),
+            )
+        )
+    ]
+    for load in loads:
+        load.start()
+    greet()
+
+    share = hidden_ref.shape[0]
+    mine = hid_t.at[pl.ds(pl.multiple_of(me_row * share, 16), share)]
+    hidden_copies = push("row", peers_of("row"), lambda i, p: hidden_ref, mine, hs_sem, hr_sem)
+    mine[...] = hidden_ref[...]
+
+    gain_t = jnp.transpose(gain_ref[...])
+    norms = norms_ref[...]
+    f_of = lax.broadcasted_iota(jnp.int32, (features, window), 0)
+    t_of = lax.broadcasted_iota(jnp.int32, (features, window), 1)
+    expand = jnp.where(t_of // heads == f_of, 1.0, 0.0).astype(bf16)
+    top = norms.astype(bf16)
+    rest = norms - top.astype(f32)
+    middle = rest.astype(bf16)
+    low = (rest - middle.astype(f32)).astype(bf16)
+    wide = (dot(top, expand) + dot(middle, expand)) + dot(low, expand)
+    row_head = lax.broadcasted_iota(jnp.int32, wide.shape, 0) % heads
+    lane_head = lax.broadcasted_iota(jnp.int32, wide.shape, 1) % heads
+    spread[...] = jnp.where(row_head == lane_head, wide, 0.0)
+
+    row_ids = lax.broadcasted_iota(jnp.int32, (tokens, tokens), 0)
+    lane_ids = lax.broadcasted_iota(jnp.int32, (tokens, tokens), 1)
+    linked = jnp.logical_or(parent_ref[...] == lane_ids, row_ids == lane_ids)
+    reached = jnp.where(linked, 1.0, 0.0)
+    for repeat in range(max(1, (nodes - 1).bit_length())):
+        reached_low = reached.astype(bf16)
+        reached = jnp.minimum(dot(reached_low, reached_low), 1.0)
+
+    for copy in hidden_copies:
+        copy.wait_recv()
+    total = jnp.zeros((1, tokens), f32)
+    for j in range(width // 128):
+        x = hid_t[128 * j : 128 * j + 128, :].astype(f32)
+        total += jnp.sum(x * x, axis=0, keepdims=True)
+    inverse = lax.rsqrt(total / width + epsilon)
+    for j in range(width // 128):
+        x = hid_t[128 * j : 128 * j + 128, :].astype(f32)
+        normed[128 * j : 128 * j + 128, :] = (x * inverse * gain_t[:, j : j + 1]).astype(bf16)
+    loads[0].wait()
+    q_mine[...] = dot(wq[...], normed[...]).astype(bf16)
+    q_copies = push("col", peers_of("col"), lambda i, p: q_mine, q_all.at[me_col], qs_sem, qr_sem)
+    q_all[me_col] = q_mine[...]
+    loads[1].wait()
+    k_mine[...] = dot(wk[...], normed[...]).astype(bf16)
+    loads[2].wait()
+    v_mine[...] = dot(wv[...], normed[...]).astype(bf16)
+    for copy in q_copies:
+        copy.wait()
+
+    cuts = [(lo, min(lo + 384, window)) for lo in range(0, window, 384)]
+    lane_feature = lax.broadcasted_iota(jnp.int32, (1, window), 1) // heads
+    lane_scale = feature_scale(lane_feature, feat_width)
+
+    def features_of(home, carry):
+        ext = extended(q_all[home], heads)
+        for lo, hi in cuts:
+            a = dot(ext, first_ref[:, lo:hi], (0, 0))
+            b = dot(ext, second_ref[:, lo:hi], (0, 0))
+            phi = a * b * lane_scale[:, lo:hi]
+            for r in range(requests):
+                phi_all[home * requests + r, :, lo:hi] = phi[r * nodes : (r + 1) * nodes, :]
+        return carry
+
+    lax.fori_loop(0, col_count, features_of, 0)
+
+    loads[3].wait()
+    group = 16 // math.gcd(count, 16)
+    nums[slots] = jnp.zeros((span, 128), f32)
+
+    def slots_of(g, carry):
+        norm_rows = spread[pl.ds(pl.multiple_of(g * (group * heads), 8), group * heads), :]
+        for i in range(group):
+            slot = g * group + i
+            shift = (count * i) % 16
+            start = count * i - shift
+            owner = plan_ref[slot]
+            phi = phi_all[owner]
+            norm_row = jnp.sum(norm_rows[i * heads : (i + 1) * heads, :], axis=0, keepdims=True)
+            weighted = phi * norm_row
+            weigh = weighted[:, 0:128]
+            for lo in range(128, window, 128):
+                weigh += weighted[:, lo : lo + 128]
+            lane = lax.broadcasted_iota(jnp.int32, weigh.shape, 1) % heads
+            den = [
+                jnp.sum(jnp.where(lane == h, weigh, 0.0), axis=1, keepdims=True) for h in range(heads)
+            ]
+            if shift:
+                phi = pltpu.roll(phi, shift, 1)
+            head_of = lax.broadcasted_iota(jnp.int32, phi.shape, 1) % heads
+            num = jnp.zeros((span, value_width), f32)
+            reach = -(-(count + shift) // 16) * 16
+            for lo, hi in [(lo, min(lo + 384, reach)) for lo in range(0, reach, 384)]:
+                masked = jnp.concatenate(
+                    [
+                        jnp.where(head_of[:, lo:hi] == h, phi[:, lo:hi], 0.0).astype(bf16)
+                        for h in range(heads)
+                    ],
+                    axis=0,
+                )
+                rows = pl.ds(pl.multiple_of(g * (group * count) + start + lo, 16), hi - lo)
+                num += dot(masked, states[rows, :])
+            nums[slot, :, 0:value_width] = num
+            nums[slot, :, value_width : value_width + 1] = jnp.concatenate(den, axis=0)
+        return carry
+
+    lax.fori_loop(0, slots // group, slots_of, 0)
+
+    def home_sum(home, request):
+        acc = jnp.zeros((span, 128), f32)
+        for k in range(capacity):
+            place = slots + home * capacity + k
+            slot = plan_ref[place]
+            wanted = jnp.full((span, 128), plan_ref[col_count * capacity + place], jnp.int32)
+            acc += jnp.where(wanted == request, nums[slot], 0.0)
+        return acc
+
+    for chip in range(chips):
+        for r in range(requests):
+            pair_out[chip, r * span : (r + 1) * span, :] = home_sum(2 * chip + (1 - me_core), r).astype(bf16)
+    pair_copies = push(
+        "col", [2 * me_chip + (1 - me_core)], lambda i, p: pair_out, pair_in, bs_sem, br_sem
+    )
+
+    k_ext = extended(k_mine[...], heads)
+    tree_num, tree_den = [], []
+    for h in range(heads):
+        at = slice(h * feat_width, (h + 1) * feat_width)
+        scaled = dot(q_mine[at, :], k_mine[at, :], (0, 0)) / math.sqrt(feat_width)
+        kernel = (1.0 + scaled + 0.5 * scaled * scaled) * reached
+        tree_den.append(jnp.sum(kernel, axis=1, keepdims=True))
+        tree_num.append(
+            dot(kernel.astype(bf16), v_mine[h * value_width : (h + 1) * value_width, :], (1, 1))
+        )
+    for copy in pair_copies:
+        copy.wait()
+
+    def combined(chip, r):
+        got = pair_in[chip, r * span : (r + 1) * span, :].astype(f32)
+        return home_sum(2 * chip + me_core, r) + got
+
+    chip_peers = [lax.rem(me_chip + step, chips) for step in range(1, chips)]
+    chip_copies = []
+    for step, chip in enumerate(chip_peers):
+        for r in range(requests):
+            chip_out[step, r * span : (r + 1) * span, :] = combined(chip, r).astype(bf16)
+        copy = pltpu.make_async_remote_copy(
+            src_ref=chip_out.at[step],
+            dst_ref=chip_in.at[step],
+            send_sem=cs_sem.at[step],
+            recv_sem=cr_sem.at[step],
+            device_id={"col": 2 * chip + me_core},
+            device_id_type=pl.DeviceIdType.MESH,
+        )
+        copy.start()
+        chip_copies.append(copy)
+    pref = [combined(me_chip, r) for r in range(requests)]
+
+    for j in range(width // 128):
+        block = hid_t[128 * j : 128 * j + 128, :].astype(f32)
+        hid[:, 128 * j : 128 * j + 128] = jnp.transpose(block)
+
+    path = dot(chosen_ref[...], reached.astype(bf16))
+    path_low = path.astype(bf16)
+    stride = first_h_ref.shape[0] // heads
+    for h in range(heads):
+        at = slice(h * stride, (h + 1) * stride)
+        feature = lax.broadcasted_iota(jnp.int32, (stride, tokens), 0)
+        phi = dot(first_h_ref[at, :], k_ext) * dot(second_h_ref[at, :], k_ext)
+        phi = phi * feature_scale(feature, feat_width)
+        high = phi.astype(bf16)
+        low = (phi - high.astype(f32)).astype(bf16)
+        norm = dot(path_low, high, (1, 1)) + dot(path_low, low, (1, 1))
+        for r in range(requests):
+            norms_out[r * heads + h : r * heads + h + 1, :] = norm[r : r + 1, 0:features]
+    phi = dot(first_t_ref[...], k_ext) * dot(second_t_ref[...], k_ext)
+    t = lax.broadcasted_iota(jnp.int32, phi.shape, 0)
+    high = (phi * feature_scale(t // heads, feat_width)).astype(bf16).astype(f32)
+    for h in range(heads):
+        values = v_mine[h * value_width : (h + 1) * value_width, :].astype(f32)
+        stacked[h * tokens : (h + 1) * tokens, :] = jnp.transpose(values).astype(bf16)
+    for r in range(requests):
+        weighted = high * path[r : r + 1, :]
+        wide = jnp.concatenate(
+            [jnp.where(t % heads == h, weighted, 0.0).astype(bf16) for h in range(heads)], axis=1
+        )
+        page = dot(wide, stacked[...])
+        states_out[r * count : (r + 1) * count, :] = page[0:count, :].astype(bf16)
+
+    for copy in chip_copies:
+        copy.wait()
+    for step in range(chips - 1):
+        for r in range(requests):
+            pref[r] += chip_in[step, r * span : (r + 1) * span, :].astype(f32)
+    loads[4].wait()
+    partial = jnp.zeros((tokens, width), f32)
+    for h in range(heads):
+        rows = jnp.concatenate([pref[r][h * nodes : (h + 1) * nodes, :] for r in range(requests)], axis=0)
+        num = rows[:, 0:value_width] + tree_num[h]
+        den = rows[:, value_width : value_width + 1] + tree_den[h]
+        mixed = (num / den).astype(bf16)
+        partial += dot(mixed, wout[h * value_width : (h + 1) * value_width, :])
+    sums[...] = partial.astype(bf16)
+
+    token_share = tokens // row_count
+    rows_of = lambda row: pl.ds(pl.multiple_of(row * token_share, 16), token_share)
+    copies = push(
+        "row", peers_of("row"), lambda i, p: sums.at[rows_of(p)], parts.at[me_row], as_sem, ar_sem
+    )
+    parts[me_row] = sums[rows_of(me_row), :]
+    for copy in copies:
+        copy.wait()
+    attn = parts[0].astype(f32)
+    for g in range(1, row_count):
+        attn += parts[g].astype(f32)
+    gathered[rows_of(me_row), :] = attn.astype(bf16)
+    mine = gathered.at[rows_of(me_row)]
+    copies = push("row", peers_of("row"), lambda i, p: mine, mine, gs_sem, gr_sem)
+    for copy in copies:
+        copy.wait()
+
+    residual = hid[...] + gathered[...].astype(f32)
+    for g in range(row_count):
+        kept[g] = residual[:, g * share : (g + 1) * share]
+    inverse = lax.rsqrt(jnp.sum(residual * residual, axis=1, keepdims=True) / width + epsilon)
+    normed_mlp = (residual * inverse * mlp_gain_ref[...]).astype(bf16)
+    loads[5].wait()
+    gate = dot(normed_mlp, wgate[...])
+    loads[6].wait()
+    up = dot(normed_mlp, wup[...])
+    active = (gate / (1.0 + jnp.exp(-gate)) * up).astype(bf16)
+    loads[7].wait()
+    mlp = dot(active, wdown[...])
+    for g in range(row_count):
+        blocks[g] = mlp[:, g * share : (g + 1) * share].astype(bf16)
+    copies = push("row", peers_of("row"), lambda i, p: blocks.at[p], arrived.at[me_row], ms_sem, mr_sem)
+    arrived[me_row] = blocks[me_row]
+    for copy in copies:
+        copy.wait()
+    final = kept[me_row]
+    for g in range(row_count):
+        final += arrived[g].astype(f32)
+    for lo in range(0, share, 128):
+        hi = min(lo + 128, share)
+        out_ref[lo:hi, :] = jnp.transpose(final[:, lo:hi]).astype(bf16)
+    for copy in hidden_copies:
+        copy.wait_send()
+
+
+def kernel_local(
+    hidden_in, attn_gain, mlp_gain, w_query, w_key, w_value, w_out, w_gate, w_up, w_down,
+    page_states, page_norms, page_home, page_request, parents, accepted,
+):
+    slots, heads, features, value_width = page_states.shape
+    feat_width = w_query.shape[1] // heads
+    requests, nodes = parents.shape
+    tokens, share = hidden_in.shape
+    width = w_gate.shape[0]
+    rows, cols = lax.axis_size("row"), lax.axis_size("col")
+    capacity = max(2, 2 * slots // cols)
+    bf16, f32 = jnp.bfloat16, jnp.float32
+    vmem = pl.BlockSpec(memory_space=pltpu.VMEM)
+    smem = pl.BlockSpec(memory_space=pltpu.SMEM)
+    hbm = pl.BlockSpec(memory_space=pl.ANY)
+    dma = pltpu.SemaphoreType.DMA
+    unit = heads * feat_width
+    span = heads * nodes
+    count = heads * features
+    window = -(-(count + 16) // 128) * 128
+
+    homes, slot_ids = page_home[:, 0], jnp.arange(slots, dtype=jnp.int32)
+    before = (homes[:, None] == homes[None, :]) & (slot_ids[None, :] < slot_ids[:, None])
+    places = homes * capacity + jnp.sum(before.astype(jnp.int32), axis=1)
+    taken = places[None, :] == jnp.arange(cols * capacity, dtype=jnp.int32)[:, None]
+    table = slots + jnp.sum(jnp.where(taken, slot_ids[None, :] - slots, 0), axis=1)
+    wanted = jnp.sum(jnp.where(taken, page_request[None, :], 0), axis=1)
+    plan = jnp.concatenate([homes * requests + page_request, table, wanted]).astype(jnp.int32)
+
+    state_rows = jnp.transpose(page_states, (0, 2, 1, 3)).reshape(slots * count, value_width)
+    parent_rows = (parents + nodes * jnp.arange(requests, dtype=jnp.int32)[:, None]).reshape(tokens, 1)
+    accepted_rows = accepted + nodes * jnp.arange(requests, dtype=jnp.int32)
+    chosen = jnp.arange(tokens, dtype=jnp.int32)[None, :] == accepted_rows[:, None]
+    chosen = jnp.pad(chosen.astype(bf16), ((0, 16 - requests), (0, 0)))
+    first, second = picks(heads, feat_width, lambda f, h: f * heads + h, window)
+    stride = -(-features // 16) * 16
+    first_h, second_h = picks(heads, feat_width, lambda f, h: h * stride + f, heads * stride)
+    constants = [jnp.asarray(c, bf16) for c in (first.T, second.T, first, second, first_h, second_h)]
+    token_share = tokens // rows
+    chips = cols // 2
+    hidden_out, state_out, norm_out = pl.pallas_call(
+        functools.partial(layer_kernel, heads, feat_width, features, value_width, requests, capacity),
+        out_shape=(
+            jax.ShapeDtypeStruct((share, tokens), bf16),
+            jax.ShapeDtypeStruct((requests * count, value_width), bf16),
+            jax.ShapeDtypeStruct((requests * heads, features), f32),
+        ),
+        in_specs=[smem] + [vmem] * 12 + [hbm] * 8,
+        out_specs=(vmem,) * 3,
+        scratch_shapes=[
+            pltpu.VMEM((unit, width), bf16),
+            pltpu.VMEM((unit, width), bf16),
+            pltpu.VMEM((heads * value_width, width), bf16),
+            pltpu.VMEM(state_rows.shape, bf16),
+            pltpu.VMEM(w_out.shape, bf16),
+            pltpu.VMEM(w_gate.shape, bf16),
+            pltpu.VMEM(w_up.shape, bf16),
+            pltpu.VMEM(w_down.shape, bf16),
+            pltpu.VMEM((width, tokens), bf16),
+            pltpu.VMEM((width, tokens), bf16),
+            pltpu.VMEM((unit, tokens), bf16),
+            pltpu.VMEM((cols, unit, tokens), bf16),
+            pltpu.VMEM((unit, tokens), bf16),
+            pltpu.VMEM((heads * value_width, tokens), bf16),
+            pltpu.VMEM((slots * heads, window), f32),
+            pltpu.VMEM((cols * requests, nodes, window), f32),
+            pltpu.VMEM((slots + 1, span, 128), f32),
+            pltpu.VMEM((chips, requests * span, 128), bf16),
+            pltpu.VMEM((chips, requests * span, 128), bf16),
+            pltpu.VMEM((chips - 1, requests * span, 128), bf16),
+            pltpu.VMEM((chips - 1, requests * span, 128), bf16),
+            pltpu.VMEM((tokens, width), f32),
+            pltpu.VMEM((heads * tokens, value_width), bf16),
+            pltpu.VMEM((tokens, width), bf16),
+            pltpu.VMEM((rows, token_share, width), bf16),
+            pltpu.VMEM((tokens, width), bf16),
+            pltpu.VMEM((rows, tokens, share), bf16),
+            pltpu.VMEM((rows, tokens, share), f32),
+            pltpu.VMEM((rows, tokens, share), bf16),
+            dma((8,)),
+            dma((rows - 1,)),
+            dma((rows - 1,)),
+            dma((cols - 1,)),
+            dma((cols - 1,)),
+            dma((1,)),
+            dma((1,)),
+            dma((chips - 1,)),
+            dma((chips - 1,)),
+        ]
+        + [dma((rows - 1,))] * 6,
+        compiler_params=pltpu.CompilerParams(
+            collective_id=0, has_side_effects=True, vmem_limit_bytes=58 * 1024 * 1024
+        ),
+        name="layer",
+    )(
+        plan, hidden_in.T, attn_gain.reshape(width // 128, 128), mlp_gain.reshape(1, width),
+        page_norms.reshape(slots * heads, features), parent_rows, chosen, *constants,
+        w_query.T, w_key.T, w_value.T, state_rows, w_out, w_gate, w_up, w_down,
+    )
+    new_states = jnp.transpose(state_out.reshape(requests, features, heads, value_width), (0, 2, 1, 3))
+    return (hidden_out.T, new_states, norm_out.reshape(requests, heads, features))
+
+
+def kernels_fit(*arrays):
+    hidden_in, w_query, page_states, parents = arrays[0], arrays[3], arrays[10], arrays[14]
+    slots, heads, features, value_width = page_states.shape
+    tokens, rows = hidden_in.shape[0], lax.axis_size("row")
+    group = 16 // math.gcd(heads * features, 16)
+    return (
+        tokens == 128
+        and tokens % (16 * rows) == 0
+        and hidden_in.shape[1] % 16 == 0
+        and 128 % heads == 0
+        and (group == 1 or 16 % heads == 0)
+        and (group * heads) % 8 == 0
+        and w_query.shape[1] + heads <= 128
+        and value_width < 128
+        and value_width % 16 == 0
+        and slots % group == 0
+        and parents.shape[0] <= 16
+        and lax.axis_size("col") % 2 == 0
+        and lax.axis_size("col") > 2
+    )
+
+
+def on_device(*arrays):
+    return kernel_local(*arrays) if kernels_fit(*arrays) else local(*arrays)
+
 
 def solution(mesh):
     return jax.shard_map(
-        local,
+        on_device,
         mesh=mesh,
         in_specs=(
             P("col", "row"),

time: 255 us -> 88.6 us (0.35); the launches traced: 251 us -> 88.2 us
  waiting for transfers between devices: 87.2 us -> 0 us
  matrix products: 81.5 us -> 0 us
  Pallas kernels: 0 us -> 74 us
  local copies, waits for them, and re-layouts: 28.5 us -> 8.54 us
  blocking collectives: 16.6 us -> 0 us
  between operations: 14.8 us -> 0.65 us
  starting transfers between devices: 13.6 us -> 0 us
  other arithmetic: 8.38 us -> 5.04 us
    dot_general x26 -> x0, matrix products: 81.5 us -> none  [the longest x1 16.1 us: local(): jnp.einsum('pnhf,phf->pnh', phi_full, got_norms, precision=highest)]
    pallas_call x0 -> x1, Pallas kernels: none -> 74 us  [kernel_local(): pl.pallas_call(functools.partial(layer_kernel, heads, feat_width, feature...]
    psum x1 -> x0, waiting for transfers between devices: 36 us -> none  [local(): lax.psum(partial_value.astype(jnp.bfloat16), 'row').astype(jnp.float32)]
    all_to_all x3 -> x0, waiting for transfers between devices: 34.1 us -> none  [the longest x1 31.5 us: local(): lax.all_to_all(sent_states, 'col', split_axis=0, concat_axis=0, tiled=True)]
    unnamed x3 -> x0, waiting for transfers between devices: 17.1 us -> none
    all_gather x1 -> x0, blocking collectives: 16.6 us -> none  [local(): gathered = lax.all_gather(hidden_in, 'row', axis=1, tiled=True)]
    all_to_all x3 -> x0, starting transfers between devices: 13.5 us -> none  [the longest x1 5.17 us: local(): lax.all_to_all(packed_ids.astype(jnp.bfloat16), 'col', split_axis=0, conc...]
    convert_element_type x4 -> x0, local copies, waits for them, and re-layouts: 11.2 us -> none  [the longest x1 10.4 us: local(): sent_states = jnp.einsum('ps,shfd->phfd', packer.astype(jnp.bfloat16), pa...]
  transfers between devices with their start and end apart: 5 -> 0, of which waited for: 4 -> 0; matrix products, arithmetic and copies ran while one was open for 29% -> 0% of each run, Pallas kernels for 0% -> 0%
where the time goes in v2:
time: 88.6 us; the launch traced here: 88.2 us
  Pallas kernels  74 us (84%)
  local copies, waits for them, and re-layouts  8.54 us (10%)
  other arithmetic  5.04 us (6%)
    pallas_call x1, Pallas kernels, kernel_local(): pl.pallas_call(functools.partial(layer_kernel, heads, feat_width, feature...  74 us
    unnamed x2, local copies, waits for them, and re-layouts  3.6 us

profile of v2, /device:TPU:0, one launch (start us, length us, event | category | flops | bytes accessed | tf_op | source)
XLA Modules:
  0.0 88.2 jit_solution(5414285805966486535)
XLA Ops:
  0.6 0.7 fusion.1
  1.3 0.1 iota_compare_fusion.2
  1.4 0.9 %convert_reduce_fusion = s32[16]{0:T(128)S(1)} fusion(s32[16]{0:T(128)} %bitcast.23), kind=kLoop, calls=%fused_computation.3 | loop fusion | flops 1264 | bytes 128 | tf_op jit(solution)/shard_map/reduce_sum | solution.py:553
  2.3 0.8 broadcast_add_fusion
  3.0 0.7 multiply_add_fusion.1
  3.7 0.7 select_reduce_fusion.1
  4.5 0.6 pad_add_fusion.plan_ref
  5.1 0.6 pad_convert_fusion.chosen_ref
  5.7 1.3 %reshape.49.mlp_gain_ref = f32[1,1792]{1,0:T(1,128)} reshape(f32[1792]{0:T(1024)} %param.24) | data formatting | bytes 14336 | tf_op jit(solution)/shard_map/reshape | solution.py:625
  7.0 0.8 reshape.55.parent_ref
  7.7 1.6 %reshape.50.norms_ref = f32[64,273]{1,0:T(8,128)} reshape(f32[16,4,273]{2,1,0:T(4,128)} %param.33) | data formatting | bytes 139776 | tf_op jit(solution)/shard_map/reshape | solution.py:626
  9.3 74.0 %layer.1 = (bf16[448,128]{1,0:T(8,128)(2,1)}, bf16[2184,112]{1,0:T(8,128)(2,1)}, f32[8,273]{1,0:T(8,128)}) custom-call(s32[80]{0:T(128)} %pad_add_fusion.plan_ref, bf16[448,128]{1,0:T(8,128)(2,1)} %bitcast.21, f32[14,128]{1,0:T(8,128)} %bitcast.22, f32[1,1792]{1,0:T(1,128)} %reshape.49.mlp_gain_ref, f32[64,273]{1,0:T(8,128)} %reshape.50.norms_ref, ...), custom_call_target="tpu_custom_call" | custom-call | tf_op jit(solution)/shard_map/layer/pallas_call | solution.py:570
  83.3 1.3 %reshape.54 = f32[2,4,273]{2,1,0:T(4,128)} reshape(f32[8,273]{1,0:T(8,128)} %get-tuple-element.8) | data formatting | bytes 17472 | tf_op jit(solution)/shard_map/reshape | solution.py:630
  84.6 1.6 %copy.29 = bf16[128,448]{0,1:T(8,128)(2,1)} copy(bf16[128,448]{0,1:T(8,128)(2,1)} %bitcast.20) | data formatting | bytes 229376
  86.2 2.0 %copy.30 = bf16[2,4,273,112]{3,1,2,0:T(4,128)(2,1)} copy(bf16[2,4,273,112]{3,1,2,0:T(4,128)(2,1)} %bitcast.17) | data formatting | bytes 978432
  (2 shorter events, 0.0 us)

commit v3 on v2

--- a/solution.py
+++ b/solution.py
@@ -213,14 +213,14 @@
     pl.semaphore_wait(barrier, count)
 
 
-def push(axis, peers, source_of, target, send_sem, recv_sem):
+def push(axis, peers, source_of, target, send_sem, recv_sem, base=0):
     copies = []
     for step, peer in enumerate(peers):
         copy = pltpu.make_async_remote_copy(
             src_ref=source_of(step, peer),
             dst_ref=target,
-            send_sem=send_sem.at[step],
-            recv_sem=recv_sem.at[step],
+            send_sem=send_sem.at[base + step],
+            recv_sem=recv_sem.at[base + step],
             device_id={axis: peer},
             device_id_type=pl.DeviceIdType.MESH,
         )
@@ -244,11 +244,12 @@
 
 def layer_kernel(
     heads, feat_width, features, value_width, requests, capacity,
-    plan_ref, hidden_ref, gain_ref, mlp_gain_ref, norms_ref, parent_ref, chosen_ref,
-    first_ref, second_ref, first_t_ref, second_t_ref, first_h_ref, second_h_ref,
+    home_ref, request_ref, accepted_ref, hidden_ref, gain_ref, mlp_gain_ref, norms_ref, parent_ref,
+    first_any, second_any, first_t_any, second_t_any, first_h_any, second_h_any,
     wq_any, wk_any, wv_any, states_any, wout_any, wgate_any, wup_any, wdown_any,
     out_ref, states_out, norms_out,
     wq, wk, wv, states, wout, wgate, wup, wdown,
+    first_ref, second_ref, first_t_ref, second_t_ref, first_h_ref, second_h_ref, table, norms_flat, normed_mlp,
     hid_t, normed, q_mine, q_all, k_mine, v_mine, spread, phi_all, nums,
     pair_out, pair_in, chip_out, chip_in,
     hid, stacked, sums, parts, gathered, blocks, kept, arrived,
@@ -266,18 +267,21 @@
     span = heads * nodes
     count = heads * features
     window = phi_all.shape[2]
-    slots = norms_ref.shape[0] // heads
+    slots = norms_ref.shape[0]
     loads = [
         pltpu.make_async_copy(src, dst, w_sem.at[i])
         for i, (src, dst) in enumerate(
             (
                 (wq_any, wq), (wk_any, wk), (wv_any, wv), (states_any, states),
                 (wout_any, wout), (wgate_any, wgate), (wup_any, wup), (wdown_any, wdown),
+                (first_any, first_ref), (second_any, second_ref),
+                (first_t_any, first_t_ref), (second_t_any, second_t_ref),
+                (first_h_any, first_h_ref), (second_h_any, second_h_ref),
             )
         )
     ]
-    for load in loads:
-        load.start()
+    for i in (0, 1, 2, 8, 9, 3, 10, 11, 12, 13, 4, 5, 6, 7):
+        loads[i].start()
     greet()
 
     share = hidden_ref.shape[0]
@@ -286,7 +290,9 @@
     mine[...] = hidden_ref[...]
 
     gain_t = jnp.transpose(gain_ref[...])
-    norms = norms_ref[...]
+    for slot in range(slots):
+        norms_flat[slot * heads : (slot + 1) * heads, :] = norms_ref[slot]
+    norms = norms_flat[...]
     f_of = lax.broadcasted_iota(jnp.int32, (features, window), 0)
     t_of = lax.broadcasted_iota(jnp.int32, (features, window), 1)
     expand = jnp.where(t_of // heads == f_of, 1.0, 0.0).astype(bf16)
@@ -301,11 +307,28 @@
 
     row_ids = lax.broadcasted_iota(jnp.int32, (tokens, tokens), 0)
     lane_ids = lax.broadcasted_iota(jnp.int32, (tokens, tokens), 1)
-    linked = jnp.logical_or(parent_ref[...] == lane_ids, row_ids == lane_ids)
+    parent_row = jnp.concatenate(
+        [parent_ref[r : r + 1, :] + r * nodes for r in range(requests)], axis=1
+    )
+    linked = jnp.logical_or(parent_row == row_ids, row_ids == lane_ids)
     reached = jnp.where(linked, 1.0, 0.0)
     for repeat in range(max(1, (nodes - 1).bit_length())):
         reached_low = reached.astype(bf16)
         reached = jnp.minimum(dot(reached_low, reached_low), 1.0)
+    reached = jnp.transpose(reached)
+
+    homes = [home_ref[slot] for slot in range(slots)]
+    places = []
+    for slot in range(slots):
+        rank = jnp.int32(0)
+        for earlier in range(slot):
+            rank += (homes[earlier] == homes[slot]).astype(jnp.int32)
+        places.append(homes[slot] * capacity + rank)
+    for place in range(col_count * capacity):
+        found = jnp.int32(slots)
+        for slot in range(slots):
+            found += (places[slot] == place).astype(jnp.int32) * (slot - slots)
+        table[place] = found
 
     for copy in hidden_copies:
         copy.wait_recv()
@@ -328,6 +351,8 @@
     for copy in q_copies:
         copy.wait()
 
+    loads[8].wait()
+    loads[9].wait()
     cuts = [(lo, min(lo + 384, window)) for lo in range(0, window, 384)]
     lane_feature = lax.broadcasted_iota(jnp.int32, (1, window), 1) // heads
     lane_scale = feature_scale(lane_feature, feat_width)
@@ -354,7 +379,7 @@
             slot = g * group + i
             shift = (count * i) % 16
             start = count * i - shift
-            owner = plan_ref[slot]
+            owner = home_ref[slot] * requests + request_ref[slot]
             phi = phi_all[owner]
             norm_row = jnp.sum(norm_rows[i * heads : (i + 1) * heads, :], axis=0, keepdims=True)
             weighted = phi * norm_row
@@ -389,9 +414,8 @@
     def home_sum(home, request):
         acc = jnp.zeros((span, 128), f32)
         for k in range(capacity):
-            place = slots + home * capacity + k
-            slot = plan_ref[place]
-            wanted = jnp.full((span, 128), plan_ref[col_count * capacity + place], jnp.int32)
+            slot = table[home * capacity + k]
+            wanted = jnp.full((span, 128), request_ref[jnp.minimum(slot, slots - 1)], jnp.int32)
             acc += jnp.where(wanted == request, nums[slot], 0.0)
         return acc
 
@@ -421,26 +445,28 @@
 
     chip_peers = [lax.rem(me_chip + step, chips) for step in range(1, chips)]
     chip_copies = []
-    for step, chip in enumerate(chip_peers):
-        for r in range(requests):
-            chip_out[step, r * span : (r + 1) * span, :] = combined(chip, r).astype(bf16)
-        copy = pltpu.make_async_remote_copy(
-            src_ref=chip_out.at[step],
-            dst_ref=chip_in.at[step],
-            send_sem=cs_sem.at[step],
-            recv_sem=cr_sem.at[step],
-            device_id={"col": 2 * chip + me_core},
-            device_id_type=pl.DeviceIdType.MESH,
-        )
-        copy.start()
-        chip_copies.append(copy)
+    for r in range(requests):
+        for step, chip in enumerate(chip_peers):
+            chip_out[r, step] = combined(chip, r).astype(bf16)
+            chip_copies += push(
+                "col", [2 * chip + me_core], lambda i, p: chip_out.at[r, step], chip_in.at[r, step],
+                cs_sem, cr_sem, r * (chips - 1) + step,
+            )
     pref = [combined(me_chip, r) for r in range(requests)]
 
     for j in range(width // 128):
         block = hid_t[128 * j : 128 * j + 128, :].astype(f32)
         hid[:, 128 * j : 128 * j + 128] = jnp.transpose(block)
 
-    path = dot(chosen_ref[...], reached.astype(bf16))
+    for i in range(10, 14):
+        loads[i].wait()
+    pick_row = lax.broadcasted_iota(jnp.int32, (16, tokens), 0)
+    pick_lane = lax.broadcasted_iota(jnp.int32, (16, tokens), 1)
+    chosen = jnp.zeros((16, tokens), f32)
+    for r in range(requests):
+        hit = jnp.logical_and(pick_row == r, pick_lane == accepted_ref[r] + r * nodes)
+        chosen = jnp.where(hit, 1.0, chosen)
+    path = dot(chosen.astype(bf16), reached.astype(bf16))
     path_low = path.astype(bf16)
     stride = first_h_ref.shape[0] // heads
     for h in range(heads):
@@ -452,7 +478,7 @@
         low = (phi - high.astype(f32)).astype(bf16)
         norm = dot(path_low, high, (1, 1)) + dot(path_low, low, (1, 1))
         for r in range(requests):
-            norms_out[r * heads + h : r * heads + h + 1, :] = norm[r : r + 1, 0:features]
+            norms_out[r, h : h + 1, :] = norm[r : r + 1, 0:features]
     phi = dot(first_t_ref[...], k_ext) * dot(second_t_ref[...], k_ext)
     t = lax.broadcasted_iota(jnp.int32, phi.shape, 0)
     high = (phi * feature_scale(t // heads, feat_width)).astype(bf16).astype(f32)
@@ -467,59 +493,86 @@
         page = dot(wide, stacked[...])
         states_out[r * count : (r + 1) * count, :] = page[0:count, :].astype(bf16)
 
-    for copy in chip_copies:
-        copy.wait()
-    for step in range(chips - 1):
-        for r in range(requests):
-            pref[r] += chip_in[step, r * span : (r + 1) * span, :].astype(f32)
+    token_share = nodes // row_count
+    steps = row_count - 1
+    row_peers = peers_of("row")
+    rows_of = lambda row: pl.ds(pl.multiple_of(row * token_share, 16), token_share)
     loads[4].wait()
-    partial = jnp.zeros((tokens, width), f32)
-    for h in range(heads):
-        rows = jnp.concatenate([pref[r][h * nodes : (h + 1) * nodes, :] for r in range(requests)], axis=0)
-        num = rows[:, 0:value_width] + tree_num[h]
-        den = rows[:, value_width : value_width + 1] + tree_den[h]
-        mixed = (num / den).astype(bf16)
-        partial += dot(mixed, wout[h * value_width : (h + 1) * value_width, :])
-    sums[...] = partial.astype(bf16)
-
-    token_share = tokens // row_count
-    rows_of = lambda row: pl.ds(pl.multiple_of(row * token_share, 16), token_share)
-    copies = push(
-        "row", peers_of("row"), lambda i, p: sums.at[rows_of(p)], parts.at[me_row], as_sem, ar_sem
-    )
-    parts[me_row] = sums[rows_of(me_row), :]
-    for copy in copies:
-        copy.wait()
-    attn = parts[0].astype(f32)
-    for g in range(1, row_count):
-        attn += parts[g].astype(f32)
-    gathered[rows_of(me_row), :] = attn.astype(bf16)
-    mine = gathered.at[rows_of(me_row)]
-    copies = push("row", peers_of("row"), lambda i, p: mine, mine, gs_sem, gr_sem)
-    for copy in copies:
-        copy.wait()
-
-    residual = hid[...] + gathered[...].astype(f32)
-    for g in range(row_count):
-        kept[g] = residual[:, g * share : (g + 1) * share]
-    inverse = lax.rsqrt(jnp.sum(residual * residual, axis=1, keepdims=True) / width + epsilon)
-    normed_mlp = (residual * inverse * mlp_gain_ref[...]).astype(bf16)
-    loads[5].wait()
-    gate = dot(normed_mlp, wgate[...])
-    loads[6].wait()
-    up = dot(normed_mlp, wup[...])
-    active = (gate / (1.0 + jnp.exp(-gate)) * up).astype(bf16)
-    loads[7].wait()
-    mlp = dot(active, wdown[...])
-    for g in range(row_count):
-        blocks[g] = mlp[:, g * share : (g + 1) * share].astype(bf16)
-    copies = push("row", peers_of("row"), lambda i, p: blocks.at[p], arrived.at[me_row], ms_sem, mr_sem)
-    arrived[me_row] = blocks[me_row]
-    for copy in copies:
-        copy.wait()
-    final = kept[me_row]
-    for g in range(row_count):
-        final += arrived[g].astype(f32)
+    sum_copies = []
+    for r in range(requests):
+        for step in range(chips - 1):
+            chip_copies[r * (chips - 1) + step].wait()
+            pref[r] += chip_in[r, step].astype(f32)
+        partial = jnp.zeros((nodes, width), f32)
+        for h in range(heads):
+            rows = pref[r][h * nodes : (h + 1) * nodes, :]
+            at = slice(r * nodes, (r + 1) * nodes)
+            num = rows[:, 0:value_width] + tree_num[h][at, :]
+            den = rows[:, value_width : value_width + 1] + tree_den[h][at, :]
+            mixed = (num / den).astype(bf16)
+            partial += dot(mixed, wout[h * value_width : (h + 1) * value_width, :])
+        sums[r] = partial.astype(bf16)
+        sum_copies.append(
+            push(
+                "row", row_peers, lambda i, p: sums.at[r, rows_of(p)], parts.at[r, me_row],
+                as_sem, ar_sem, r * steps,
+            )
+        )
+        parts[r, me_row] = sums[r, rows_of(me_row), :]
+
+    gather_copies = []
+    for r in range(requests):
+        for copy in sum_copies[r]:
+            copy.wait()
+        attn = parts[r, 0].astype(f32)
+        for g in range(1, row_count):
+            attn += parts[r, g].astype(f32)
+        gathered[r, rows_of(me_row), :] = attn.astype(bf16)
+        mine = gathered.at[r, rows_of(me_row)]
+        gather_copies.append(
+            push("row", row_peers, lambda i, p: mine, mine, gs_sem, gr_sem, r * steps)
+        )
+
+    mlp_copies = []
+    for r in range(requests):
+        for copy in gather_copies[r]:
+            copy.wait()
+        residual = hid[r * nodes : (r + 1) * nodes, :] + gathered[r].astype(f32)
+        for g in range(row_count):
+            kept[r, g] = residual[:, g * share : (g + 1) * share]
+        inverse = lax.rsqrt(jnp.sum(residual * residual, axis=1, keepdims=True) / width + epsilon)
+        for j in range(width // 128):
+            at = slice(128 * j, 128 * j + 128)
+            scaled = residual[:, at] * inverse * mlp_gain_ref[j : j + 1, :]
+            normed_mlp[r, :, at] = scaled.astype(bf16)
+        if r == 0:
+            loads[5].wait()
+        gate = dot(normed_mlp[r], wgate[...])
+        if r == 0:
+            loads[6].wait()
+        up = dot(normed_mlp[r], wup[...])
+        active = (gate / (1.0 + jnp.exp(-gate)) * up).astype(bf16)
+        if r == 0:
+            loads[7].wait()
+        mlp = dot(active, wdown[...])
+        for g in range(row_count):
+            blocks[r, g] = mlp[:, g * share : (g + 1) * share].astype(bf16)
+        mlp_copies.append(
+            push(
+                "row", row_peers, lambda i, p: blocks.at[r, p], arrived.at[r, me_row],
+                ms_sem, mr_sem, r * steps,
+            )
+        )
+        arrived[r, me_row] = blocks[r, me_row]
+    finals = []
+    for r in range(requests):
+        for copy in mlp_copies[r]:
+            copy.wait()
+        final = kept[r, me_row]
+        for g in range(row_count):
+            final += arrived[r, g].astype(f32)
+        finals.append(final)
+    final = jnp.concatenate(finals, axis=0)
     for lo in range(0, share, 128):
         hi = min(lo + 128, share)
         out_ref[lo:hi, :] = jnp.transpose(final[:, lo:hi]).astype(bf16)
@@ -548,33 +601,21 @@
     count = heads * features
     window = -(-(count + 16) // 128) * 128
 
-    homes, slot_ids = page_home[:, 0], jnp.arange(slots, dtype=jnp.int32)
-    before = (homes[:, None] == homes[None, :]) & (slot_ids[None, :] < slot_ids[:, None])
-    places = homes * capacity + jnp.sum(before.astype(jnp.int32), axis=1)
-    taken = places[None, :] == jnp.arange(cols * capacity, dtype=jnp.int32)[:, None]
-    table = slots + jnp.sum(jnp.where(taken, slot_ids[None, :] - slots, 0), axis=1)
-    wanted = jnp.sum(jnp.where(taken, page_request[None, :], 0), axis=1)
-    plan = jnp.concatenate([homes * requests + page_request, table, wanted]).astype(jnp.int32)
-
     state_rows = jnp.transpose(page_states, (0, 2, 1, 3)).reshape(slots * count, value_width)
-    parent_rows = (parents + nodes * jnp.arange(requests, dtype=jnp.int32)[:, None]).reshape(tokens, 1)
-    accepted_rows = accepted + nodes * jnp.arange(requests, dtype=jnp.int32)
-    chosen = jnp.arange(tokens, dtype=jnp.int32)[None, :] == accepted_rows[:, None]
-    chosen = jnp.pad(chosen.astype(bf16), ((0, 16 - requests), (0, 0)))
     first, second = picks(heads, feat_width, lambda f, h: f * heads + h, window)
     stride = -(-features // 16) * 16
     first_h, second_h = picks(heads, feat_width, lambda f, h: h * stride + f, heads * stride)
     constants = [jnp.asarray(c, bf16) for c in (first.T, second.T, first, second, first_h, second_h)]
-    token_share = tokens // rows
+    token_share = nodes // rows
     chips = cols // 2
     hidden_out, state_out, norm_out = pl.pallas_call(
         functools.partial(layer_kernel, heads, feat_width, features, value_width, requests, capacity),
         out_shape=(
             jax.ShapeDtypeStruct((share, tokens), bf16),
             jax.ShapeDtypeStruct((requests * count, value_width), bf16),
-            jax.ShapeDtypeStruct((requests * heads, features), f32),
+            jax.ShapeDtypeStruct((requests, heads, features), f32),
         ),
-        in_specs=[smem] + [vmem] * 12 + [hbm] * 8,
+        in_specs=[smem] * 3 + [vmem] * 5 + [hbm] * 14,
         out_specs=(vmem,) * 3,
         scratch_shapes=[
             pltpu.VMEM((unit, width), bf16),
@@ -585,6 +626,12 @@
             pltpu.VMEM(w_gate.shape, bf16),
             pltpu.VMEM(w_up.shape, bf16),
             pltpu.VMEM(w_down.shape, bf16),
+        ]
+        + [pltpu.VMEM(c.shape, bf16) for c in constants]
+        + [
+            pltpu.SMEM((cols * capacity,), jnp.int32),
+            pltpu.VMEM((slots * heads, features), f32),
+            pltpu.VMEM((requests, nodes, width), bf16),
             pltpu.VMEM((width, tokens), bf16),
             pltpu.VMEM((width, tokens), bf16),
             pltpu.VMEM((unit, tokens), bf16),
@@ -596,38 +643,38 @@
             pltpu.VMEM((slots + 1, span, 128), f32),
             pltpu.VMEM((chips, requests * span, 128), bf16),
             pltpu.VMEM((chips, requests * span, 128), bf16),
-            pltpu.VMEM((chips - 1, requests * span, 128), bf16),
-            pltpu.VMEM((chips - 1, requests * span, 128), bf16),
+            pltpu.VMEM((requests, chips - 1, span, 128), bf16),
+            pltpu.VMEM((requests, chips - 1, span, 128), bf16),
             pltpu.VMEM((tokens, width), f32),
             pltpu.VMEM((heads * tokens, value_width), bf16),
-            pltpu.VMEM((tokens, width), bf16),
-            pltpu.VMEM((rows, token_share, width), bf16),
-            pltpu.VMEM((tokens, width), bf16),
-            pltpu.VMEM((rows, tokens, share), bf16),
-            pltpu.VMEM((rows, tokens, share), f32),
-            pltpu.VMEM((rows, tokens, share), bf16),
-            dma((8,)),
+            pltpu.VMEM((requests, nodes, width), bf16),
+            pltpu.VMEM((requests, rows, token_share, width), bf16),
+            pltpu.VMEM((requests, nodes, width), bf16),
+            pltpu.VMEM((requests, rows, nodes, share), bf16),
+            pltpu.VMEM((requests, rows, nodes, share), f32),
+            pltpu.VMEM((requests, rows, nodes, share), bf16),
+            dma((14,)),
             dma((rows - 1,)),
             dma((rows - 1,)),
             dma((cols - 1,)),
             dma((cols - 1,)),
             dma((1,)),
             dma((1,)),
-            dma((chips - 1,)),
-            dma((chips - 1,)),
+            dma((requests * (chips - 1),)),
+            dma((requests * (chips - 1),)),
         ]
-        + [dma((rows - 1,))] * 6,
+        + [dma((requests * (rows - 1),))] * 6,
         compiler_params=pltpu.CompilerParams(
             collective_id=0, has_side_effects=True, vmem_limit_bytes=58 * 1024 * 1024
         ),
         name="layer",
     )(
-        plan, hidden_in.T, attn_gain.reshape(width // 128, 128), mlp_gain.reshape(1, width),
-        page_norms.reshape(slots * heads, features), parent_rows, chosen, *constants,
+        page_home[:, 0], page_request, accepted, hidden_in.T, attn_gain.reshape(width // 128, 128),
+        mlp_gain.reshape(width // 128, 128), page_norms, parents, *constants,
         w_query.T, w_key.T, w_value.T, state_rows, w_out, w_gate, w_up, w_down,
     )
     new_states = jnp.transpose(state_out.reshape(requests, features, heads, value_width), (0, 2, 1, 3))
-    return (hidden_out.T, new_states, norm_out.reshape(requests, heads, features))
+    return (hidden_out.T, new_states, norm_out)
 
 
 def kernels_fit(*arrays):
@@ -637,7 +684,7 @@
     group = 16 // math.gcd(heads * features, 16)
     return (
         tokens == 128
-        and tokens % (16 * rows) == 0
+        and parents.shape[1] % (16 * rows) == 0
         and hidden_in.shape[1] % 16 == 0
         and 128 % heads == 0
         and (group == 1 or 16 % heads == 0)

time: 88.6 us -> 75.2 us (0.85)
  other arithmetic: 5.04 us -> 0 us
  Pallas kernels: 74 us -> 69.3 us
  local copies, waits for them, and re-layouts: 8.54 us -> 4.91 us
    reshape x4 -> x0, local copies, waits for them, and re-layouts: 4.94 us -> none  [the longest x1 1.57 us: kernel_local(): page_norms.reshape(slots * heads, features)]
    pallas_call x1, Pallas kernels: 74 us -> 69.3 us  [kernel_local(): pl.pallas_call(functools.partial(layer_kernel, heads, feat_width, feature...]
    add x4 -> x0, other arithmetic: 2.09 us -> none  [the longest x1 0.75 us: kernel_local(): parents + nodes * jnp.arange(requests, dtype=jnp.int32)[:, None]]
    reduce_sum x2 -> x0, other arithmetic: 1.65 us -> none  [the longest x1 0.91 us: kernel_local(): places = homes * capacity + jnp.sum(before.astype(jnp.int32), axis=1)]
    unnamed x2 -> x3, local copies, waits for them, and re-layouts: 3.6 us -> 4.91 us
where the time goes in v3:
time: 75.2 us; the launch traced here: 74.9 us
  Pallas kernels  69.3 us (92%)
  local copies, waits for them, and re-layouts  4.91 us (7%)
    pallas_call x1, Pallas kernels, kernel_local(): pl.pallas_call(functools.partial(layer_kernel, heads, feat_width, feature...  69.3 us
    unnamed x3, local copies, waits for them, and re-layouts  4.91 us

profile of v3, /device:TPU:0, one launch (start us, length us, event | category | flops | bytes accessed | tf_op | source)
XLA Modules:
  0.0 74.9 jit_solution(9644021103019740176)
XLA Ops:
  0.6 69.3 %layer.1 = (bf16[448,128]{1,0:T(8,128)(2,1)}, bf16[2184,112]{1,0:T(8,128)(2,1)}, f32[2,4,273]{2,1,0:T(4,128)}) custom-call(s32[16]{0:T(128)} %bitcast.23, s32[16]{0:T(128)} %request_ref.1, s32[2]{0:T(128)} %accepted_ref.1, bf16[448,128]{1,0:T(8,128)(2,1)} %bitcast.20, f32[14,128]{1,0:T(8,128)} %bitcast.21, f32[14,128]{1,0:T(8,128)} %bitcast.22, ...), custom_call_target="tpu_custom_call" | custom-call | tf_op jit(solution)/shard_map/layer/pallas_call | solution.py:611
  70.0 1.6 %copy.28 = bf16[128,448]{0,1:T(8,128)(2,1)} copy(bf16[128,448]{0,1:T(8,128)(2,1)} %bitcast.19) | data formatting | bytes 229376
  71.5 2.0 %copy.29 = bf16[2,4,273,112]{3,1,2,0:T(4,128)(2,1)} copy(bf16[2,4,273,112]{3,1,2,0:T(4,128)(2,1)} %bitcast.16) | data formatting | bytes 978432
  73.6 1.3 %copy.30 = f32[2,4,273]{2,1,0:T(4,128)} copy(f32[2,4,273]{2,1,0:T(4,128)} %get-tuple-element.14) | data formatting | bytes 17472

commit v4 on v3

--- a/solution.py
+++ b/solution.py
@@ -201,7 +201,7 @@
     return [lax.rem(me + step, size) for step in range(1, size)]
 
 
-def greet():
+def greet(between):
     barrier = pltpu.get_barrier_semaphore()
     count = 0
     for axis in MESH_KEYS:
@@ -210,6 +210,7 @@
                 barrier, inc=1, device_id={axis: peer}, device_id_type=pl.DeviceIdType.MESH
             )
             count += 1
+    between()
     pl.semaphore_wait(barrier, count)
 
 
@@ -249,7 +250,7 @@
     wq_any, wk_any, wv_any, states_any, wout_any, wgate_any, wup_any, wdown_any,
     out_ref, states_out, norms_out,
     wq, wk, wv, states, wout, wgate, wup, wdown,
-    first_ref, second_ref, first_t_ref, second_t_ref, first_h_ref, second_h_ref, table, norms_flat, normed_mlp,
+    first_ref, second_ref, first_t_ref, second_t_ref, first_h_ref, second_h_ref, table, norms_flat, normed_mlp, head_mask,
     hid_t, normed, q_mine, q_all, k_mine, v_mine, spread, phi_all, nums,
     pair_out, pair_in, chip_out, chip_in,
     hid, stacked, sums, parts, gathered, blocks, kept, arrived,
@@ -280,9 +281,12 @@
             )
         )
     ]
-    for i in (0, 1, 2, 8, 9, 3, 10, 11, 12, 13, 4, 5, 6, 7):
-        loads[i].start()
-    greet()
+
+    def start_loads():
+        for i in (0, 1, 2, 8, 9, 3, 10, 11, 12, 13, 4, 5, 6, 7):
+            loads[i].start()
+
+    greet(start_loads)
 
     share = hidden_ref.shape[0]
     mine = hid_t.at[pl.ds(pl.multiple_of(me_row * share, 16), share)]
@@ -316,6 +320,10 @@
         reached_low = reached.astype(bf16)
         reached = jnp.minimum(dot(reached_low, reached_low), 1.0)
     reached = jnp.transpose(reached)
+
+    mask_lane = lax.broadcasted_iota(jnp.int32, (nodes, window), 1) % heads
+    for h in range(heads):
+        head_mask[h] = jnp.where(mask_lane == h, 1.0, 0.0).astype(bf16)
 
     homes = [home_ref[slot] for slot in range(slots)]
     places = []
@@ -348,8 +356,10 @@
     k_mine[...] = dot(wk[...], normed[...]).astype(bf16)
     loads[2].wait()
     v_mine[...] = dot(wv[...], normed[...]).astype(bf16)
-    for copy in q_copies:
-        copy.wait()
+    for j in range(width // 128):
+        block = hid_t[128 * j : 128 * j + 128, :].astype(f32)
+        hid[:, 128 * j : 128 * j + 128] = jnp.transpose(block)
+
 
     loads[8].wait()
     loads[9].wait()
@@ -357,7 +367,7 @@
     lane_feature = lax.broadcasted_iota(jnp.int32, (1, window), 1) // heads
     lane_scale = feature_scale(lane_feature, feat_width)
 
-    def features_of(home, carry):
+    def features_of(home):
         ext = extended(q_all[home], heads)
         for lo, hi in cuts:
             a = dot(ext, first_ref[:, lo:hi], (0, 0))
@@ -365,9 +375,11 @@
             phi = a * b * lane_scale[:, lo:hi]
             for r in range(requests):
                 phi_all[home * requests + r, :, lo:hi] = phi[r * nodes : (r + 1) * nodes, :]
-        return carry
-
-    lax.fori_loop(0, col_count, features_of, 0)
+
+    features_of(me_col)
+    for step, copy in enumerate(q_copies):
+        copy.wait()
+        features_of(lax.rem(me_col + col_count - (step + 1), col_count))
 
     loads[3].wait()
     group = 16 // math.gcd(count, 16)
@@ -392,16 +404,12 @@
             ]
             if shift:
                 phi = pltpu.roll(phi, shift, 1)
-            head_of = lax.broadcasted_iota(jnp.int32, phi.shape, 1) % heads
+            phi = phi.astype(bf16)
             num = jnp.zeros((span, value_width), f32)
             reach = -(-(count + shift) // 16) * 16
             for lo, hi in [(lo, min(lo + 384, reach)) for lo in range(0, reach, 384)]:
                 masked = jnp.concatenate(
-                    [
-                        jnp.where(head_of[:, lo:hi] == h, phi[:, lo:hi], 0.0).astype(bf16)
-                        for h in range(heads)
-                    ],
-                    axis=0,
+                    [phi[:, lo:hi] * head_mask[h, :, lo:hi] for h in range(heads)], axis=0
                 )
                 rows = pl.ds(pl.multiple_of(g * (group * count) + start + lo, 16), hi - lo)
                 num += dot(masked, states[rows, :])
@@ -454,9 +462,32 @@
             )
     pref = [combined(me_chip, r) for r in range(requests)]
 
-    for j in range(width // 128):
-        block = hid_t[128 * j : 128 * j + 128, :].astype(f32)
-        hid[:, 128 * j : 128 * j + 128] = jnp.transpose(block)
+    token_share = nodes // row_count
+    steps = row_count - 1
+    row_peers = peers_of("row")
+    rows_of = lambda row: pl.ds(pl.multiple_of(row * token_share, 16), token_share)
+    loads[4].wait()
+    sum_copies = []
+    for r in range(requests):
+        for step in range(chips - 1):
+            chip_copies[r * (chips - 1) + step].wait()
+            pref[r] += chip_in[r, step].astype(f32)
+        partial = jnp.zeros((nodes, width), f32)
+        for h in range(heads):
+            rows = pref[r][h * nodes : (h + 1) * nodes, :]
+            at = slice(r * nodes, (r + 1) * nodes)
+            num = rows[:, 0:value_width] + tree_num[h][at, :]
+            den = rows[:, value_width : value_width + 1] + tree_den[h][at, :]
+            mixed = (num / den).astype(bf16)
+            partial += dot(mixed, wout[h * value_width : (h + 1) * value_width, :])
+        sums[r] = partial.astype(bf16)
+        sum_copies.append(
+            push(
+                "row", row_peers, lambda i, p: sums.at[r, rows_of(p)], parts.at[r, me_row],
+                as_sem, ar_sem, r * steps,
+            )
+        )
+        parts[r, me_row] = sums[r, rows_of(me_row), :]
 
     for i in range(10, 14):
         loads[i].wait()
@@ -485,7 +516,7 @@
     for h in range(heads):
         values = v_mine[h * value_width : (h + 1) * value_width, :].astype(f32)
         stacked[h * tokens : (h + 1) * tokens, :] = jnp.transpose(values).astype(bf16)
-    for r in range(requests):
+    def accepted_page(r):
         weighted = high * path[r : r + 1, :]
         wide = jnp.concatenate(
             [jnp.where(t % heads == h, weighted, 0.0).astype(bf16) for h in range(heads)], axis=1
@@ -493,32 +524,7 @@
         page = dot(wide, stacked[...])
         states_out[r * count : (r + 1) * count, :] = page[0:count, :].astype(bf16)
 
-    token_share = nodes // row_count
-    steps = row_count - 1
-    row_peers = peers_of("row")
-    rows_of = lambda row: pl.ds(pl.multiple_of(row * token_share, 16), token_share)
-    loads[4].wait()
-    sum_copies = []
-    for r in range(requests):
-        for step in range(chips - 1):
-            chip_copies[r * (chips - 1) + step].wait()
-            pref[r] += chip_in[r, step].astype(f32)
-        partial = jnp.zeros((nodes, width), f32)
-        for h in range(heads):
-            rows = pref[r][h * nodes : (h + 1) * nodes, :]
-            at = slice(r * nodes, (r + 1) * nodes)
-            num = rows[:, 0:value_width] + tree_num[h][at, :]
-            den = rows[:, value_width : value_width + 1] + tree_den[h][at, :]
-            mixed = (num / den).astype(bf16)
-            partial += dot(mixed, wout[h * value_width : (h + 1) * value_width, :])
-        sums[r] = partial.astype(bf16)
-        sum_copies.append(
-            push(
-                "row", row_peers, lambda i, p: sums.at[r, rows_of(p)], parts.at[r, me_row],
-                as_sem, ar_sem, r * steps,
-            )
-        )
-        parts[r, me_row] = sums[r, rows_of(me_row), :]
+    accepted_page(0)
 
     gather_copies = []
     for r in range(requests):
@@ -532,6 +538,9 @@
         gather_copies.append(
             push("row", row_peers, lambda i, p: mine, mine, gs_sem, gr_sem, r * steps)
         )
+
+    for r in range(1, requests):
+        accepted_page(r)
 
     mlp_copies = []
     for r in range(requests):
@@ -632,6 +641,7 @@
             pltpu.SMEM((cols * capacity,), jnp.int32),
             pltpu.VMEM((slots * heads, features), f32),
             pltpu.VMEM((requests, nodes, width), bf16),
+            pltpu.VMEM((heads, nodes, window), bf16),
             pltpu.VMEM((width, tokens), bf16),
             pltpu.VMEM((width, tokens), bf16),
             pltpu.VMEM((unit, tokens), bf16),

time: 75.2 us -> 75.1 us (level)
  no operation moved by 1% of the time
where the time goes in v4:
time: 75.1 us; the launch traced here: 74.9 us
  Pallas kernels  69.3 us (92%)
  local copies, waits for them, and re-layouts  4.91 us (7%)
    pallas_call x1, Pallas kernels, kernel_local(): pl.pallas_call(functools.partial(layer_kernel, heads, feat_width, feature...  69.3 us
    unnamed x3, local copies, waits for them, and re-layouts  4.91 us

profile of v4, /device:TPU:0, one launch (start us, length us, event | category | flops | bytes accessed | tf_op | source)
XLA Modules:
  0.0 74.9 jit_solution(4360360811385584997)
XLA Ops:
  0.6 69.3 %layer.1 = (bf16[448,128]{1,0:T(8,128)(2,1)}, bf16[2184,112]{1,0:T(8,128)(2,1)}, f32[2,4,273]{2,1,0:T(4,128)}) custom-call(s32[16]{0:T(128)} %bitcast.23, s32[16]{0:T(128)} %request_ref.1, s32[2]{0:T(128)} %accepted_ref.1, bf16[448,128]{1,0:T(8,128)(2,1)} %bitcast.20, f32[14,128]{1,0:T(8,128)} %bitcast.21, f32[14,128]{1,0:T(8,128)} %bitcast.22, ...), custom_call_target="tpu_custom_call" | custom-call | tf_op jit(solution)/shard_map/layer/pallas_call | solution.py:620
  69.9 1.6 %copy.28 = bf16[128,448]{0,1:T(8,128)(2,1)} copy(bf16[128,448]{0,1:T(8,128)(2,1)} %bitcast.19) | data formatting | bytes 229376
  71.5 2.0 %copy.29 = bf16[2,4,273,112]{3,1,2,0:T(4,128)(2,1)} copy(bf16[2,4,273,112]{3,1,2,0:T(4,128)(2,1)} %bitcast.16) | data formatting | bytes 978432
  73.5 1.3 %copy.30 = f32[2,4,273]{2,1,0:T(4,128)} copy(f32[2,4,273]{2,1,0:T(4,128)} %get-tuple-element.14) | data formatting | bytes 17472
